TPU v7x, 512 devices: a whole 4x4x16 slice. The times are simulated.
512 devices in a mesh: normal: 16 (over z), span: 8 (over x, core), stream: 4 (over y).
Axes of the slice: x: 4, y: 4, z: 16, core: 2. Of those that a mesh axis runs over, the one named last changes fastest.
Arguments:
- iterate: float32 [768, 5, 8, 512], P('normal', None, 'span', 'stream'), may hold values from -6 to 6
- source: float32 [768, 5, 8, 512], P('normal', None, 'span', 'stream'), may hold values from -6 to 6
- pivot: float32 [768, 5, 5, 8, 512], P('normal', None, None, 'span', 'stream'), as said below
- lower: float32 [768, 5, 5, 8, 512], P('normal', None, None, 'span', 'stream'), as said below
- upper: float32 [768, 5, 5, 8, 512], P('normal', None, None, 'span', 'stream'), as said below
- coupling: float32 [4, 768, 5, 5, 8, 512], P(None, 'normal', None, None, 'span', 'stream'), may hold values from -0.6 to 0.6
- iblank: int32 [768, 8, 512], P('normal', 'span', 'stream'), may hold values from 0 to 2
- donor: int32 [768, 8, 512], P('normal', 'span', 'stream'), may hold values from 0 to 6143
Outputs:
- smoothed: float32 [768, 5, 8, 512], P('normal', None, 'span', 'stream')
Inputs may be any that keep to these rules, and one draw needn't show every extreme that they name: `donor`: an offset within a tile of 48 x 1 x 128 points. pivot blocks are full 5x5 blocks. lower and upper factor blocks are full 5x5 blocks; the recurrences stay bounded. upper factor blocks are full 5x5 blocks.
All inputs are finite; a program needn't handle non-finite values.
Results may differ from a plain program's by a relative error of at most 0.00018.
Values sent between devices are 32-bit elements; how exact they have to be, the bound alone decides.
No kernel may reach another device: no remote copies, remote signals or barrier semaphores. Data moves between devices by JAX's collectives and lax.ppermute only.
A program may use at most 64 MiB of HBM per device.

v0:
```python
import functools

import jax
import jax.numpy as jnp
from jax import lax
from jax.experimental import pallas as pl
from jax.experimental.pallas import tpu as pltpu
from jax.sharding import PartitionSpec as P

COMP = 5
BLOCK = COMP * COMP
PIECES = 8
LANES = 128
STEPS = 6
POINTS = PIECES * STEPS
SIZES = range(COMP)
FWD0, FWD1, FWD2, BWD0, BWD1, BWD2, FOLD, HEAD, FROM_Y, FROM_X = range(10)
MAPS = 10
ROWS = 3 * BLOCK
VALUES = 2 * COMP
PADDED = 88
VMEM = pl.BlockSpec(memory_space=pltpu.VMEM)


def vector_at(ref, step):
    return [ref[pl.ds(step * COMP + c, PIECES, stride=STEPS * COMP), :] for c in SIZES]


def block_at(ref, step, base=0):
    start = base + step * BLOCK
    return [
        [ref[pl.ds(start + c * COMP + e, PIECES, stride=STEPS * BLOCK), :] for e in SIZES]
        for c in SIZES
    ]


def packed_at(ref, step):
    return [ref[pl.ds((step * COMP + c) * PIECES, PIECES), :] for c in SIZES]


def put_packed(ref, step, value):
    for c in SIZES:
        ref[pl.ds((step * COMP + c) * PIECES, PIECES), :] = value[c]


def map_at(ref, which):
    return [
        [ref[pl.ds(((which * COMP + c) * COMP + e) * PIECES, PIECES), :] for e in SIZES]
        for c in SIZES
    ]


def put_map(ref, which, value):
    for c in SIZES:
        for e in SIZES:
            ref[pl.ds(((which * COMP + c) * COMP + e) * PIECES, PIECES), :] = value[c][e]


def total(terms):
    while len(terms) > 1:
        terms = [sum(terms[k : k + 2][1:], terms[k]) for k in range(0, len(terms), 2)]
    return terms[0]


def times(block, vector):
    return [total([block[c][e] * vector[e] for e in SIZES]) for c in SIZES]


def product(left, right):
    return [
        [total([left[c][k] * right[k][e] for k in SIZES]) for e in SIZES] for c in SIZES
    ]


def each(function, *maps):
    return [[function(*(m[c][e] for m in maps)) for e in SIZES] for c in SIZES]


def add(left, right):
    return [a + b for a, b in zip(left, right)]


def less(left, right):
    return [a - b for a, b in zip(left, right)]


def moved(value, steps):
    return pltpu.roll(value, steps % PIECES, 0)


def donate(x_ref, donor_ref, donated_ref):
    lanes, rows = [], []
    for step in range(STEPS):
        place = donor_ref[pl.ds(step, PIECES, stride=STEPS), :]
        lanes.append(place & (LANES - 1))
        rows.append(place >> 7)

    def body(row, found):
        found = list(found)
        values = [
            jnp.broadcast_to(x_ref[pl.ds(row * COMP + c, 1), :], (PIECES, LANES)) for c in SIZES
        ]
        for step in range(STEPS):
            here = rows[step] == row
            for c in SIZES:
                picked = jnp.take_along_axis(
                    values[c], lanes[step], axis=1, mode="promise_in_bounds"
                )
                at = step * COMP + c
                found[at] = jnp.where(here, picked, found[at])
        return tuple(found)

    zero = jnp.zeros((PIECES, LANES), jnp.float32)
    found = lax.fori_loop(0, POINTS, body, (zero,) * (STEPS * COMP))
    for at in range(STEPS * COMP):
        donated_ref[pl.ds(at * PIECES, PIECES), :] = found[at]


def donate_kernel(x_ref, donor_ref, donated_ref):
    donate(x_ref, donor_ref, donated_ref)


def maps_kernel(lower_ref, upper_ref, maps_ref, whole_ref, local_ref):
    piece = lax.broadcasted_iota(jnp.int32, (PIECES, LANES), 0)
    one = jnp.ones((PIECES, LANES), jnp.float32)
    zero = jnp.zeros((PIECES, LANES), jnp.float32)
    eye = [[one if c == e else zero for e in SIZES] for c in SIZES]

    def pack(value):
        return tuple(value[c][e] for c in SIZES for e in SIZES)

    def unpack(flat):
        return [list(flat[c * COMP : (c + 1) * COMP]) for c in SIZES]

    first = each(lambda a: -a, block_at(lower_ref, 0))
    put_map(local_ref, 0, first)

    def forward(step, state):
        block = block_at(lower_ref, step)
        state = each(lambda a: -a, product(block, unpack(state)))
        put_map(local_ref, step, state)
        return pack(state)

    ahead = unpack(lax.fori_loop(1, STEPS, forward, pack(first)))

    def backward(count, carry):
        behind, fold = unpack(carry[:BLOCK]), unpack(carry[BLOCK:])
        step = STEPS - 1 - count
        block = block_at(upper_ref, step)
        behind = each(lambda a: -a, product(block, behind))
        fold = each(lambda a, b: a - b, map_at(local_ref, step), product(block, fold))
        return pack(behind) + pack(fold)

    last = block_at(upper_ref, STEPS - 1)
    start = pack(each(lambda a: -a, last)) + pack(map_at(local_ref, STEPS - 1))
    carry = lax.fori_loop(1, STEPS, backward, start)
    behind, fold = unpack(carry[:BLOCK]), unpack(carry[BLOCK:])
    put_map(maps_ref, FOLD, fold)

    window = ahead
    for level, shift in enumerate((1, 2, 4)):
        inside = piece >= shift
        put_map(maps_ref, FWD0 + level, each(lambda a: jnp.where(inside, a, 0.0), window))
        longer = product(window, each(lambda a: moved(a, shift), window))
        window = each(lambda a, b: jnp.where(inside, a, b), longer, window)
    head = each(lambda a, b: jnp.where(piece == 0, b, moved(a, 1)), window, eye)
    put_map(maps_ref, HEAD, head)
    for c in SIZES:
        for e in SIZES:
            whole_ref[pl.ds(c * COMP + e, 1), :] = window[c][e][PIECES - 1 :, :]

    window = behind
    response = product(fold, head)
    for level, shift in enumerate((1, 2, 4)):
        inside = piece < PIECES - shift
        masked = each(lambda a: jnp.where(inside, a, 0.0), window)
        put_map(maps_ref, BWD0 + level, masked)
        response = each(
            lambda a, b: a + b,
            response,
            product(masked, each(lambda a: moved(a, -shift), response)),
        )
        longer = product(window, each(lambda a: moved(a, -shift), window))
        window = each(lambda a, b: jnp.where(inside, a, b), longer, window)
    final = piece == PIECES - 1
    put_map(maps_ref, FROM_Y, each(lambda a: jnp.where(final, 0.0, moved(a, -1)), response))
    put_map(maps_ref, FROM_X, each(lambda a, b: jnp.where(final, b, moved(a, -1)), window, eye))
    for c in SIZES:
        for e in SIZES:
            at = c * COMP + e
            whole_ref[pl.ds(BLOCK + at, 1), :] = response[c][e][:1, :]
            whole_ref[pl.ds(2 * BLOCK + at, 1), :] = window[c][e][:1, :]


def solve_kernel(
    copies,
    x_ref,
    below_ref,
    above_ref,
    left_ref,
    right_ref,
    source_ref,
    pivot_ref,
    lower_ref,
    upper_ref,
    coupling_ref,
    iblank_ref,
    donated_ref,
    maps_ref,
    whole_ref,
    sent_ref,
    scaled_ref,
    starts_ref,
    states_ref,
):
    lane = lax.broadcasted_iota(jnp.int32, (PIECES, LANES), 1)
    piece = lax.broadcasted_iota(jnp.int32, (PIECES, LANES), 0)
    zero = jnp.zeros((PIECES, LANES), jnp.float32)

    def forward(step, state):
        x = vector_at(x_ref, step)
        before = [
            pltpu.roll(jnp.where(lane == LANES - 1, a, b), 1, 1)
            for a, b in zip(vector_at(left_ref, step), x)
        ]
        after = [
            pltpu.roll(jnp.where(lane == 0, a, b), LANES - 1, 1)
            for a, b in zip(vector_at(right_ref, step), x)
        ]
        near = [vector_at(below_ref, step), vector_at(above_ref, step), before, after]
        rhs = vector_at(source_ref, step)
        for direc in range(4):
            block = block_at(coupling_ref, step, direc * POINTS * BLOCK)
            for c in SIZES:
                rhs[c] = rhs[c] - total([block[e][c] * near[direc][e] for e in SIZES])
        flag = iblank_ref[pl.ds(step, PIECES, stride=STEPS), :]
        donated = packed_at(donated_ref, step)
        rhs = [
            jnp.where(flag == 0, 0.0, a + jnp.where(flag == 2, b, 0.0))
            for a, b in zip(rhs, donated)
        ]
        scaled = times(block_at(pivot_ref, step), rhs)
        put_packed(scaled_ref, step, scaled)
        state = less(scaled, times(block_at(lower_ref, step), state))
        put_packed(states_ref, step, state)
        return tuple(state)

    ahead = list(lax.fori_loop(0, STEPS, forward, (zero,) * COMP))

    def backward(count, state):
        step = STEPS - 1 - count
        y = packed_at(states_ref, step)
        return tuple(less(y, times(block_at(upper_ref, step), state)))

    behind = list(lax.fori_loop(0, STEPS, backward, (zero,) * COMP))

    for level, shift in enumerate((1, 2, 4)):
        ahead = add(ahead, times(map_at(maps_ref, FWD0 + level), [moved(a, shift) for a in ahead]))
    entry = [jnp.where(piece == 0, 0.0, moved(a, 1)) for a in ahead]
    behind = add(behind, times(map_at(maps_ref, FOLD), entry))
    for level, shift in enumerate((1, 2, 4)):
        behind = add(
            behind, times(map_at(maps_ref, BWD0 + level), [moved(a, -shift) for a in behind])
        )
    put_packed(starts_ref, 0, entry)
    put_packed(
        starts_ref, 1, [jnp.where(piece == PIECES - 1, 0.0, moved(a, -1)) for a in behind]
    )
    if whole_ref is not None:
        sent_ref[pl.ds(0, ROWS), :] = whole_ref[...]
        base = ROWS
        sent_ref[pl.ds(ROWS + VALUES, PADDED - ROWS - VALUES), :] = jnp.zeros(
            (PADDED - ROWS - VALUES, LANES), jnp.float32
        )
    else:
        base = 0
    for copy in range(copies):
        for c in SIZES:
            at = base + copy * VALUES + c
            sent_ref[pl.ds(at, 1), :] = ahead[c][PIECES - 1 :, :]
            sent_ref[pl.ds(at + COMP, 1), :] = behind[c][:1, :]


def solve_without(copies, *refs):
    solve_kernel(copies, *refs[:13], None, *refs[13:])


def finish_kernel(
    count,
    stride,
    offset,
    all_maps_ref,
    all_values_ref,
    lower_ref,
    upper_ref,
    maps_ref,
    scaled_ref,
    starts_ref,
    out_ref,
    states_ref,
    entry_ref,
):
    me = lax.axis_index("normal")

    def row_map(base):
        return [[all_maps_ref[pl.ds(base + c * COMP + e, 1), :] for e in SIZES] for c in SIZES]

    def row_vector(base):
        return [all_values_ref[pl.ds(base + c, 1), :] for c in SIZES]

    none = (jnp.zeros((1, LANES), jnp.float32),) * COMP

    def forward(device, state):
        for c in SIZES:
            entry_ref[pl.ds(device * PIECES + c, 1), :] = state[c]
        value = row_vector(device * stride + offset)
        return tuple(add(value, times(row_map(device * PADDED), list(state))))

    lax.fori_loop(0, count, forward, none)

    def state_of(device):
        return [entry_ref[pl.ds(device * PIECES + c, 1), :] for c in SIZES]

    def backward(step, state):
        device = count - 1 - step
        value = row_vector(device * stride + offset + COMP)
        value = add(value, times(row_map(device * PADDED + BLOCK), state_of(device)))
        return tuple(add(value, times(row_map(device * PADDED + 2 * BLOCK), list(state))))

    x_in = lax.fori_loop(0, count - 1 - me, backward, none)

    y_in = [jnp.broadcast_to(a, (PIECES, LANES)) for a in state_of(me)]
    x_in = [jnp.broadcast_to(a, (PIECES, LANES)) for a in x_in]

    y_start = add(packed_at(starts_ref, 0), times(map_at(maps_ref, HEAD), y_in))
    x_start = add(packed_at(starts_ref, 1), times(map_at(maps_ref, FROM_Y), y_in))
    x_start = add(x_start, times(map_at(maps_ref, FROM_X), x_in))

    def ahead(step, state):
        state = less(packed_at(scaled_ref, step), times(block_at(lower_ref, step), list(state)))
        put_packed(states_ref, step, state)
        return tuple(state)

    lax.fori_loop(0, STEPS, ahead, tuple(y_start))

    def behind(turn, state):
        step = STEPS - 1 - turn
        state = less(packed_at(states_ref, step), times(block_at(upper_ref, step), list(state)))
        for c in SIZES:
            out_ref[pl.ds(step * COMP + c, PIECES, stride=STEPS * COMP), :] = state[c]
        return tuple(state)

    lax.fori_loop(0, STEPS, behind, tuple(x_start))


def floats(rows):
    return jax.ShapeDtypeStruct((rows, LANES), jnp.float32)


def scratch(rows):
    return pltpu.VMEM((rows, LANES), jnp.float32)


def call(kernel, inputs, out_rows, scratch_rows, name, micros, limit=16 << 20):
    out_shape = [floats(r) for r in out_rows]
    return pl.pallas_call(
        kernel,
        out_shape=out_shape,
        in_specs=[VMEM] * len(inputs),
        out_specs=[VMEM] * len(out_rows),
        scratch_shapes=[scratch(r) for r in scratch_rows],
        compiler_params=pltpu.CompilerParams(vmem_limit_bytes=limit),
        cost_estimate=pl.CostEstimate(
            flops=0, bytes_accessed=int(micros * 3.0e6), transcendentals=0
        ),
        name=name,
    )(*inputs)


def ring(count, step):
    return [(i, (i + step) % count) for i in range(count)]


def per_device(iterate, source, pivot, lower, upper, coupling, iblank, donor):
    count = lax.axis_size("normal")
    x = iterate.reshape(-1, LANES)
    source, pivot, lower, upper, coupling, iblank, donor = (
        a.reshape(-1, LANES) for a in (source, pivot, lower, upper, coupling, iblank, donor)
    )
    field = POINTS * COMP
    state = STEPS * COMP * PIECES

    def around(x):
        return [
            lax.ppermute(x, axis, ring(lax.axis_size(axis), step))
            for axis in ("span", "stream")
            for step in (1, -1)
        ]

    near = around(x)
    maps, whole = call(
        maps_kernel, (lower, upper), (MAPS * BLOCK * PIECES, ROWS), (STEPS * BLOCK * PIECES,), "maps", 2
    )
    (donated,) = call(donate_kernel, (x, donor), (state,), (), "donate", 2)
    fixed = (source, pivot, lower, upper, coupling, iblank)
    sent, scaled, starts = call(
        functools.partial(solve_kernel, 1),
        (x, *near, *fixed, donated, maps, whole),
        (PADDED, state, 2 * COMP * PIECES),
        (state,),
        "solve",
        2,
    )
    everyone = lax.all_gather(sent, "normal", tiled=True)
    (x,) = call(
        functools.partial(finish_kernel, count, PADDED, ROWS),
        (everyone, everyone, lower, upper, maps, scaled, starts),
        (field,),
        (state, count * PIECES),
        "finish",
        2,
    )

    near = around(x)
    (donated,) = call(donate_kernel, (x, donor), (state,), (), "donate", 2)
    sent, scaled, starts = call(
        functools.partial(solve_without, count),
        (x, *near, *fixed, donated, maps),
        (count * VALUES, state, 2 * COMP * PIECES),
        (state,),
        "solve",
        2,
    )
    values = lax.all_to_all(sent.reshape(count, VALUES, 1, LANES), "normal", 0, 0)
    (x,) = call(
        functools.partial(finish_kernel, count, VALUES, 0),
        (everyone, values.reshape(-1, LANES), lower, upper, maps, scaled, starts),
        (field,),
        (state, count * PIECES),
        "finish",
        2,
    )
    return x.reshape(iterate.shape)


def solution(mesh):
    placed = (
        P("normal", None, "span", "stream"),
        P("normal", None, "span", "stream"),
        P("normal", None, None, "span", "stream"),
        P("normal", None, None, "span", "stream"),
        P("normal", None, None, "span", "stream"),
        P(None, "normal", None, None, "span", "stream"),
        P("normal", "span", "stream"),
        P("normal", "span", "stream"),
    )
    return jax.shard_map(
        per_device,
        mesh=mesh,
        in_specs=placed,
        out_specs=P("normal", None, "span", "stream"),
        check_vma=False,
    )
```

profile of v0, /device:TPU:24, one launch (start us, length us, event | category | flops | bytes accessed | tf_op | source)
XLA Modules:
  0.0 103.2 jit_solution(1533308445635931135)
XLA Ops:
  0.0 2.6 %collective-permute-start.3 = (f32[240,128]{1,0:T(8,128)}, f32[240,128]{1,0:T(8,128)S(1)}, u32[]{:S(2)}, u32[]{:S(2)}) collective-permute-start(f32[240,128]{1,0:T(8,128)} %bitcast.25), channel_id=1, source_target_pairs={{0,3},{1,0},{2,1},{3,2},{4,7},{5,4},{6,5},{7,6},{8,11},{9,8},{10,9... | collective-permute-start | bytes 368648 | tf_op jit(solution)/shard_map/ppermute | solution.py:395
  2.6 6.8 %collective-permute-start.2 = (f32[240,128]{1,0:T(8,128)}, f32[240,128]{1,0:T(8,128)S(1)}, u32[]{:S(2)}, u32[]{:S(2)}) collective-permute-start(f32[240,128]{1,0:T(8,128)} %bitcast.26), channel_id=1, source_target_pairs={{0,1},{1,2},{2,3},{3,0},{4,5},{5,6},{6,7},{7,4},{8,9},{9,10},{10,1... | collective-permute-start | bytes 368648 | tf_op jit(solution)/shard_map/ppermute | solution.py:395
  9.4 0.0 collective-permute-start.1
  9.5 0.5 collective-permute-start
  10.0 0.9 copy-done.9
  10.9 0.7 copy-done.14
  11.6 5.6 %donate.2.donated_ref = f32[240,128]{1,0:T(8,128)S(1)} custom-call(f32[240,128]{1,0:T(8,128)S(1)} %bitcast.29, s32[48,128]{1,0:T(8,128)S(1)} %bitcast.36), custom_call_target="tpu_custom_call" | custom-call | bytes 6000000 | tf_op jit(solution)/shard_map/donate/pallas_call | solution.py:366
  17.2 0.0 copy-start
  17.2 1.1 %copy-done = f32[48,5,5,1,128]{4,3,2,1,0:T(1,128)S(1)} copy-done((f32[48,5,5,1,128]{4,3,2,1,0:T(1,128)S(1)}, f32[48,5,5,1,128]{4,3,2,1,0:T(1,128)}, u32[]{:S(2)}) %copy-start) | copy-done | bytes 614424
  18.3 1.1 %copy-done.3 = f32[48,5,5,1,128]{4,3,2,1,0:T(1,128)S(1)} copy-done((f32[48,5,5,1,128]{4,3,2,1,0:T(1,128)S(1)}, f32[48,5,5,1,128]{4,3,2,1,0:T(1,128)}, u32[]{:S(2)}) %copy-start.3) | copy-done | bytes 614424
  19.4 1.0 %maps.1 = (f32[2000,128]{1,0:T(8,128)S(1)}, f32[75,128]{1,0:T(8,128)S(1)}) custom-call(f32[1200,128]{1,0:T(8,128)S(1)} %bitcast.11, f32[1200,128]{1,0:T(8,128)S(1)} %bitcast.16), custom_call_target="tpu_custom_call" | custom-call | bytes 6000000 | tf_op jit(solution)/shard_map/maps/pallas_call | solution.py:366
  20.5 0.0 copy-start.1
  20.5 1.1 %copy-done.1 = f32[48,5,5,1,128]{4,3,2,1,0:T(1,128)S(1)} copy-done((f32[48,5,5,1,128]{4,3,2,1,0:T(1,128)S(1)}, f32[48,5,5,1,128]{4,3,2,1,0:T(1,128)}, u32[]{:S(2)}) %copy-start.1) | copy-done | bytes 614424
  21.5 1.1 %copy-done.4 = f32[48,5,5,1,128]{4,3,2,1,0:T(1,128)S(1)} copy-done((f32[48,5,5,1,128]{4,3,2,1,0:T(1,128)S(1)}, f32[48,5,5,1,128]{4,3,2,1,0:T(1,128)}, u32[]{:S(2)}) %copy-start.4) | copy-done | bytes 614424
  22.6 1.7 %copy-done.5 = f32[4,48,5,5,1,128]{5,4,3,2,1,0:T(1,128)S(1)} copy-done((f32[4,48,5,5,1,128]{5,4,3,2,1,0:T(1,128)S(1)}, f32[4,48,5,5,1,128]{5,4,3,2,1,0:T(1,128)}, u32[]{:S(2)}) %copy-start.5) | copy-done | bytes 2457624
  24.3 1.1 %copy-done.7 = f32[48,5,5,1,128]{4,3,2,1,0:T(1,128)S(1)} copy-done((f32[48,5,5,1,128]{4,3,2,1,0:T(1,128)S(1)}, f32[48,5,5,1,128]{4,3,2,1,0:T(1,128)}, u32[]{:S(2)}) %copy-start.7) | copy-done | bytes 614424
  25.4 0.9 copy-done.10
  26.3 0.9 copy-done.11
  27.2 0.7 copy-done.12
  27.9 0.7 solve.2
  28.7 0.0 copy-start.6
  28.7 0.0 copy-start.8
  28.7 38.3 %all_gather.3.all_maps_ref.all_values_ref = f32[1408,128]{1,0:T(8,128)S(1)} all-gather(f32[88,128]{1,0:T(8,128)S(1)} %get-tuple-element.15), channel_id=1, replica_groups=mesh['normal'=16,'span'=8,'stream'=4] {'normal'}, dimensions={0}, use_global_device_ids=true | all-gather | bytes 765952 | tf_op jit(solution)/shard_map/all_gather | solution.py:414
  67.1 0.7 finish.2.x_ref.refs_0_
  67.8 1.9 %collective-permute-start.7 = (f32[240,128]{1,0:T(8,128)S(1)}, f32[240,128]{1,0:T(8,128)S(1)}, u32[]{:S(2)}, u32[]{:S(2)}) collective-permute-start(f32[240,128]{1,0:T(8,128)S(1)} %finish.2.x_ref.refs_0_), channel_id=1, source_target_pairs={{0,3},{1,0},{2,1},{3,2},{4,7},{5,4},{6,5},{7,6},{8,11},{9,8},{10,9... | collective-permute-start | bytes 368648 | tf_op jit(solution)/shard_map/ppermute | solution.py:395
  69.7 5.1 %collective-permute-start.6 = (f32[240,128]{1,0:T(8,128)S(1)}, f32[240,128]{1,0:T(8,128)S(1)}, u32[]{:S(2)}, u32[]{:S(2)}) collective-permute-start(f32[240,128]{1,0:T(8,128)S(1)} %finish.2.x_ref.refs_0_), channel_id=1, source_target_pairs={{0,1},{1,2},{2,3},{3,0},{4,5},{5,6},{6,7},{7,4},{8,9},{9,10},{10,1... | collective-permute-start | bytes 368648 | tf_op jit(solution)/shard_map/ppermute | solution.py:395
  74.8 0.0 collective-permute-start.5
  74.9 0.5 collective-permute-start.4
  75.4 5.6 %donate.3.refs_11_ = f32[240,128]{1,0:T(8,128)S(1)} custom-call(f32[240,128]{1,0:T(8,128)S(1)} %finish.2.x_ref.refs_0_, s32[48,128]{1,0:T(8,128)S(1)} %bitcast.37), custom_call_target="tpu_custom_call" | custom-call | bytes 6000000 | tf_op jit(solution)/shard_map/donate/pallas_call | solution.py:366
  81.1 0.8 solve.3
  81.8 20.0 %all_to_all.5 = f32[16,10,1,128]{3,2,1,0:T(1,128)S(1)} all-to-all(f32[16,10,1,128]{3,2,1,0:T(1,128)S(1)} %bitcast.38), channel_id=1, replica_groups=mesh['normal'=16,'span'=8,'stream'=4] {'normal'}, dimensions={0} | all-to-all | bytes 163840 | tf_op jit(solution)/shard_map/all_to_all | solution.py:434
  101.8 1.4 %finish.3 = f32[240,128]{1,0:T(8,128)} custom-call(f32[1408,128]{1,0:T(8,128)S(1)} %all_gather.3.all_maps_ref.all_values_ref, f32[160,128]{1,0:T(8,128)S(1)} %bitcast.33, f32[1200,128]{1,0:T(8,128)S(1)} %bitcast.15, f32[1200,128]{1,0:T(8,128)S(1)} %bitcast.20, f32[2000,128]{1,0:T(8,128)S(1)} %get-tuple-element.13.maps_ref.refs_12_, ...), custom_call_target="tpu_custom_call" | custom-call | bytes 6000000 | tf_op jit(solution)/shard_map/finish/pallas_call | solution.py:366
  (25 shorter events, 0.1 us)
Async XLA Ops:
  0.0 20.4 %collective-permute-start.3 = (f32[240,128]{1,0:T(8,128)}, f32[240,128]{1,0:T(8,128)S(1)}, u32[]{:S(2)}, u32[]{:S(2)}) collective-permute-start(f32[240,128]{1,0:T(8,128)} %bitcast.25), channel_id=1, source_target_pairs={{0,3},{1,0},{2,1},{3,2},{4,7},{5,4},{6,5},{7,6},{8,11},{9,8},{10,9... | collective-permute-start | bytes 368648 | tf_op jit(solution)/shard_map/ppermute | solution.py:395
  2.6 17.8 %collective-permute-start.2 = (f32[240,128]{1,0:T(8,128)}, f32[240,128]{1,0:T(8,128)S(1)}, u32[]{:S(2)}, u32[]{:S(2)}) collective-permute-start(f32[240,128]{1,0:T(8,128)} %bitcast.26), channel_id=1, source_target_pairs={{0,1},{1,2},{2,3},{3,0},{4,5},{5,6},{6,7},{7,4},{8,9},{9,10},{10,1... | collective-permute-start | bytes 368648 | tf_op jit(solution)/shard_map/ppermute | solution.py:395
  9.4 11.0 %collective-permute-start.1 = (f32[240,128]{1,0:T(8,128)}, f32[240,128]{1,0:T(8,128)S(1)}, u32[]{:S(2)}, u32[]{:S(2)}) collective-permute-start(f32[240,128]{1,0:T(8,128)} %bitcast.27), channel_id=1, source_target_pairs={{0,28},{4,0},{8,4},{12,8},{16,12},{20,16},{24,20},{28,24},{1,29},{... | collective-permute-start | bytes 368648 | tf_op jit(solution)/shard_map/ppermute | solution.py:395
  9.5 11.0 %collective-permute-start = (f32[240,128]{1,0:T(8,128)}, f32[240,128]{1,0:T(8,128)S(1)}, u32[]{:S(2)}, u32[]{:S(2)}) collective-permute-start(f32[240,128]{1,0:T(8,128)} %bitcast.28), channel_id=1, source_target_pairs={{0,4},{4,8},{8,12},{12,16},{16,20},{20,24},{24,28},{28,0},{1,5},{5... | collective-permute-start | bytes 368648 | tf_op jit(solution)/shard_map/ppermute | solution.py:395
  10.0 0.9 copy-start.9
  10.9 0.7 copy-start.14
  17.2 1.1 %copy-start = (f32[48,5,5,1,128]{4,3,2,1,0:T(1,128)S(1)}, f32[48,5,5,1,128]{4,3,2,1,0:T(1,128)}, u32[]{:S(2)}) copy-start(f32[48,5,5,1,128]{4,3,2,1,0:T(1,128)} %param.11) | copy-start | bytes 1843204
  18.3 1.1 %copy-start.3 = (f32[48,5,5,1,128]{4,3,2,1,0:T(1,128)S(1)}, f32[48,5,5,1,128]{4,3,2,1,0:T(1,128)}, u32[]{:S(2)}) copy-start(f32[48,5,5,1,128]{4,3,2,1,0:T(1,128)} %param.12) | copy-start | bytes 1843204
  20.5 1.1 %copy-start.1 = (f32[48,5,5,1,128]{4,3,2,1,0:T(1,128)S(1)}, f32[48,5,5,1,128]{4,3,2,1,0:T(1,128)}, u32[]{:S(2)}) copy-start(f32[48,5,5,1,128]{4,3,2,1,0:T(1,128)} %param.11) | copy-start | bytes 1843204
  21.5 1.1 %copy-start.4 = (f32[48,5,5,1,128]{4,3,2,1,0:T(1,128)S(1)}, f32[48,5,5,1,128]{4,3,2,1,0:T(1,128)}, u32[]{:S(2)}) copy-start(f32[48,5,5,1,128]{4,3,2,1,0:T(1,128)} %param.12) | copy-start | bytes 1843204
  22.6 1.7 %copy-start.5 = (f32[4,48,5,5,1,128]{5,4,3,2,1,0:T(1,128)S(1)}, f32[4,48,5,5,1,128]{5,4,3,2,1,0:T(1,128)}, u32[]{:S(2)}) copy-start(f32[4,48,5,5,1,128]{5,4,3,2,1,0:T(1,128)} %param.13) | copy-start | bytes 7372804
  24.3 1.1 %copy-start.7 = (f32[48,5,5,1,128]{4,3,2,1,0:T(1,128)S(1)}, f32[48,5,5,1,128]{4,3,2,1,0:T(1,128)}, u32[]{:S(2)}) copy-start(f32[48,5,5,1,128]{4,3,2,1,0:T(1,128)} %param.10) | copy-start | bytes 1843204
  25.4 0.9 copy-start.10
  26.3 0.9 copy-start.11
  27.2 0.7 copy-start.12
  27.9 39.1 %copy-start.2 = (f32[48,5,5,1,128]{4,3,2,1,0:T(1,128)S(1)}, f32[48,5,5,1,128]{4,3,2,1,0:T(1,128)}, u32[]{:S(2)}) copy-start(f32[48,5,5,1,128]{4,3,2,1,0:T(1,128)} %param.11) | copy-start | bytes 1843204
  28.7 46.7 %copy-start.15 = (s32[48,1,128]{2,1,0:T(1,128)S(1)}, s32[48,1,128]{2,1,0:T(1,128)}, u32[]{:S(2)}) copy-start(s32[48,1,128]{2,1,0:T(1,128)} %param.15) | copy-start | bytes 73732
  28.7 52.3 %copy-start.6 = (f32[4,48,5,5,1,128]{5,4,3,2,1,0:T(1,128)S(1)}, f32[4,48,5,5,1,128]{5,4,3,2,1,0:T(1,128)}, u32[]{:S(2)}) copy-start(f32[4,48,5,5,1,128]{5,4,3,2,1,0:T(1,128)} %param.13) | copy-start | bytes 7372804
  28.7 52.3 %copy-start.8 = (f32[48,5,5,1,128]{4,3,2,1,0:T(1,128)S(1)}, f32[48,5,5,1,128]{4,3,2,1,0:T(1,128)}, u32[]{:S(2)}) copy-start(f32[48,5,5,1,128]{4,3,2,1,0:T(1,128)} %param.10) | copy-start | bytes 1843204
  28.7 52.3 %copy-start.13 = (s32[48,1,128]{2,1,0:T(1,128)S(1)}, s32[48,1,128]{2,1,0:T(1,128)}, u32[]{:S(2)}) copy-start(s32[48,1,128]{2,1,0:T(1,128)} %param.14) | copy-start | bytes 73732
  67.8 13.2 %collective-permute-start.7 = (f32[240,128]{1,0:T(8,128)S(1)}, f32[240,128]{1,0:T(8,128)S(1)}, u32[]{:S(2)}, u32[]{:S(2)}) collective-permute-start(f32[240,128]{1,0:T(8,128)S(1)} %finish.2.x_ref.refs_0_), channel_id=1, source_target_pairs={{0,3},{1,0},{2,1},{3,2},{4,7},{5,4},{6,5},{7,6},{8,11},{9,8},{10,9... | collective-permute-start | bytes 368648 | tf_op jit(solution)/shard_map/ppermute | solution.py:395
  69.7 11.3 %collective-permute-start.6 = (f32[240,128]{1,0:T(8,128)S(1)}, f32[240,128]{1,0:T(8,128)S(1)}, u32[]{:S(2)}, u32[]{:S(2)}) collective-permute-start(f32[240,128]{1,0:T(8,128)S(1)} %finish.2.x_ref.refs_0_), channel_id=1, source_target_pairs={{0,1},{1,2},{2,3},{3,0},{4,5},{5,6},{6,7},{7,4},{8,9},{9,10},{10,1... | collective-permute-start | bytes 368648 | tf_op jit(solution)/shard_map/ppermute | solution.py:395
  74.8 6.2 %collective-permute-start.5 = (f32[240,128]{1,0:T(8,128)S(1)}, f32[240,128]{1,0:T(8,128)S(1)}, u32[]{:S(2)}, u32[]{:S(2)}) collective-permute-start(f32[240,128]{1,0:T(8,128)S(1)} %finish.2.x_ref.refs_0_), channel_id=1, source_target_pairs={{0,28},{4,0},{8,4},{12,8},{16,12},{20,16},{24,20},{28,24},{1,29},{... | collective-permute-start | bytes 368648 | tf_op jit(solution)/shard_map/ppermute | solution.py:395
  74.9 6.2 %collective-permute-start.4 = (f32[240,128]{1,0:T(8,128)S(1)}, f32[240,128]{1,0:T(8,128)S(1)}, u32[]{:S(2)}, u32[]{:S(2)}) collective-permute-start(f32[240,128]{1,0:T(8,128)S(1)} %finish.2.x_ref.refs_0_), channel_id=1, source_target_pairs={{0,4},{4,8},{8,12},{12,16},{16,20},{20,24},{24,28},{28,0},{1,5},{5... | collective-permute-start | bytes 368648 | tf_op jit(solution)/shard_map/ppermute | solution.py:395
where the time goes:
time: 104 us; the launch traced here: 103 us
  blocking collectives  58.3 us (56%)
  starting transfers between devices  17.5 us (17%)
  Pallas kernels  15.9 us (15%)
  local copies, waits for them, and re-layouts  11.3 us (11%)
    all_gather x1, blocking collectives, per_device(): everyone = lax.all_gather(sent, 'normal', tiled=True)  38.3 us
    all_to_all x1, blocking collectives, per_device(): lax.all_to_all(sent.reshape(count, VALUES, 1, LANES), 'normal', 0, 0)  20 us
    ppermute x8, starting transfers between devices, around(): lax.ppermute(x, axis, ring(lax.axis_size(axis), step))  17.5 us
    pallas_call x7, Pallas kernels, call(): pl.pallas_call(kernel, out_shape=out_shape, in_specs=[VMEM] * len(inputs)...  15.9 us
    unnamed x32, local copies, waits for them, and re-layouts  11.3 us
  transfers between devices with their start and end apart: 8, of which 0 were waited for; matrix products, arithmetic and copies ran while one was open for 0% of the time, Pallas kernels for 12%

commit v1 on v0

--- a/solution.py
+++ b/solution.py
@@ -95,32 +95,42 @@
         lanes.append(place & (LANES - 1))
         rows.append(place >> 7)
 
-    def body(row, found):
-        found = list(found)
-        values = [
-            jnp.broadcast_to(x_ref[pl.ds(row * COMP + c, 1), :], (PIECES, LANES)) for c in SIZES
-        ]
-        for step in range(STEPS):
+    zero = jnp.zeros((PIECES, LANES), jnp.float32)
+    for step in range(STEPS):
+        found = [zero] * COMP
+        for row in range(POINTS):
             here = rows[step] == row
             for c in SIZES:
-                picked = jnp.take_along_axis(
-                    values[c], lanes[step], axis=1, mode="promise_in_bounds"
-                )
-                at = step * COMP + c
-                found[at] = jnp.where(here, picked, found[at])
-        return tuple(found)
-
-    zero = jnp.zeros((PIECES, LANES), jnp.float32)
-    found = lax.fori_loop(0, POINTS, body, (zero,) * (STEPS * COMP))
-    for at in range(STEPS * COMP):
-        donated_ref[pl.ds(at * PIECES, PIECES), :] = found[at]
+                line = jnp.broadcast_to(x_ref[pl.ds(row * COMP + c, 1), :], (PIECES, LANES))
+                picked = jnp.take_along_axis(line, lanes[step], axis=1, mode="promise_in_bounds")
+                found[c] = jnp.where(here, picked, found[c])
+        put_packed(donated_ref, step, found)
 
 
 def donate_kernel(x_ref, donor_ref, donated_ref):
     donate(x_ref, donor_ref, donated_ref)
 
 
-def maps_kernel(lower_ref, upper_ref, maps_ref, whole_ref, local_ref):
+def start_kernel(*refs):
+    given, kept = refs[:8], refs[8:16]
+    donated_ref, maps_ref, whole_ref, local_ref, arrived = refs[16:]
+    copies = [
+        pltpu.make_async_copy(a, b, arrived.at[k]) for k, (a, b) in enumerate(zip(given, kept))
+    ]
+    for copy in copies:
+        copy.start()
+    lower_ref, upper_ref, x_ref, donor_ref = kept[:4]
+    for copy in copies[:2]:
+        copy.wait()
+    make_maps(lower_ref, upper_ref, maps_ref, whole_ref, local_ref)
+    for copy in copies[2:4]:
+        copy.wait()
+    donate(x_ref, donor_ref, donated_ref)
+    for copy in copies[4:]:
+        copy.wait()
+
+
+def make_maps(lower_ref, upper_ref, maps_ref, whole_ref, local_ref):
     piece = lax.broadcasted_iota(jnp.int32, (PIECES, LANES), 0)
     one = jnp.ones((PIECES, LANES), jnp.float32)
     zero = jnp.zeros((PIECES, LANES), jnp.float32)
@@ -398,10 +408,20 @@
         ]
 
     near = around(x)
-    maps, whole = call(
-        maps_kernel, (lower, upper), (MAPS * BLOCK * PIECES, ROWS), (STEPS * BLOCK * PIECES,), "maps", 2
-    )
-    (donated,) = call(donate_kernel, (x, donor), (state,), (), "donate", 2)
+    given = (lower, upper, x, donor, source, pivot, coupling, iblank)
+    shapes = [jax.ShapeDtypeStruct(a.shape, a.dtype) for a in given]
+    shapes += [floats(r) for r in (state, MAPS * BLOCK * PIECES, ROWS)]
+    *given, donated, maps, whole = pl.pallas_call(
+        start_kernel,
+        out_shape=shapes,
+        in_specs=[pl.BlockSpec(memory_space=pltpu.HBM)] * len(given),
+        out_specs=[VMEM] * len(shapes),
+        scratch_shapes=[scratch(STEPS * BLOCK * PIECES), pltpu.SemaphoreType.DMA((len(given),))],
+        compiler_params=pltpu.CompilerParams(vmem_limit_bytes=16 << 20),
+        cost_estimate=pl.CostEstimate(flops=0, bytes_accessed=12 << 20, transcendentals=0),
+        name="start",
+    )(*(pltpu.with_memory_space_constraint(a, pltpu.HBM) for a in given))
+    lower, upper, x, donor, source, pivot, coupling, iblank = given
     fixed = (source, pivot, lower, upper, coupling, iblank)
     sent, scaled, starts = call(
         functools.partial(solve_kernel, 1),

time: 104 us -> 89.9 us (0.86)
  local copies, waits for them, and re-layouts: 11.3 us -> 0 us
  Pallas kernels: 15.9 us -> 9.23 us
  waiting for transfers between devices: 0.02 us -> 4.58 us
    unnamed x32 -> x0, local copies, waits for them, and re-layouts: 11.3 us -> none
    pallas_call x7 -> x5, Pallas kernels: 15.9 us -> 5.2 us  [call(): pl.pallas_call(kernel, out_shape=out_shape, in_specs=[VMEM] * len(inputs)...]
    ppermute x8, waiting for transfers between devices: 0.02 us -> 4.58 us  [around(): lax.ppermute(x, axis, ring(lax.axis_size(axis), step))]
    pallas_call x0 -> x1, Pallas kernels: none -> 4.04 us  [per_device(): pl.pallas_call(start_kernel, out_shape=shapes, in_specs=[pl.BlockSpec(mem...]
  transfers between devices with their start and end apart: 8 -> 8, of which waited for: 0 -> 3; matrix products, arithmetic and copies ran while one was open for 0% -> 0% of each run, Pallas kernels for 12% -> 6%
where the time goes in v1:
time: 89.9 us; the launch traced here: 89.7 us
  blocking collectives  58.2 us (65%)
  starting transfers between devices  17.5 us (19%)
  Pallas kernels  9.23 us (10%)
  waiting for transfers between devices  4.58 us (5%)
    all_gather x1, blocking collectives, per_device(): everyone = lax.all_gather(sent, 'normal', tiled=True)  38.9 us
    all_to_all x1, blocking collectives, per_device(): lax.all_to_all(sent.reshape(count, VALUES, 1, LANES), 'normal', 0, 0)  19.3 us
    ppermute x8, starting transfers between devices, around(): lax.ppermute(x, axis, ring(lax.axis_size(axis), step))  17.5 us
    pallas_call x5, Pallas kernels, call(): pl.pallas_call(kernel, out_shape=out_shape, in_specs=[VMEM] * len(inputs)...  5.2 us
    ppermute x8, waiting for transfers between devices, around(): lax.ppermute(x, axis, ring(lax.axis_size(axis), step))  4.58 us
    pallas_call x1, Pallas kernels, per_device(): pl.pallas_call(start_kernel, out_shape=shapes, in_specs=[pl.BlockSpec(mem...  4.04 us
  transfers between devices with their start and end apart: 8, of which 3 were waited for; matrix products, arithmetic and copies ran while one was open for 0% of the time, Pallas kernels for 6%

profile of v1, /device:TPU:24, one launch (start us, length us, event | category | flops | bytes accessed | tf_op | source)
XLA Modules:
  0.0 89.7 jit_solution(9248588774911704666)
XLA Ops:
  0.0 2.6 %collective-permute-start.3 = (f32[240,128]{1,0:T(8,128)}, f32[240,128]{1,0:T(8,128)S(1)}, u32[]{:S(2)}, u32[]{:S(2)}) collective-permute-start(f32[240,128]{1,0:T(8,128)} %bitcast.18), channel_id=1, source_target_pairs={{0,3},{1,0},{2,1},{3,2},{4,7},{5,4},{6,5},{7,6},{8,11},{9,8},{10,9... | collective-permute-start | bytes 368648 | tf_op jit(solution)/shard_map/ppermute | solution.py:405
  2.6 6.8 %collective-permute-start.2 = (f32[240,128]{1,0:T(8,128)}, f32[240,128]{1,0:T(8,128)S(1)}, u32[]{:S(2)}, u32[]{:S(2)}) collective-permute-start(f32[240,128]{1,0:T(8,128)} %bitcast.19), channel_id=1, source_target_pairs={{0,1},{1,2},{2,3},{3,0},{4,5},{5,6},{6,7},{7,4},{8,9},{9,10},{10,1... | collective-permute-start | bytes 368648 | tf_op jit(solution)/shard_map/ppermute | solution.py:405
  9.4 0.0 collective-permute-start.1
  9.5 0.5 collective-permute-start
  9.9 4.0 %start.1 = (f32[1200,128]{1,0:T(8,128)S(1)}, f32[1200,128]{1,0:T(8,128)S(1)}, f32[240,128]{1,0:T(8,128)S(1)}, s32[48,128]{1,0:T(8,128)S(1)}, f32[240,128]{1,0:T(...) custom-call(f32[1200,128]{1,0:T(8,128)} %bitcast.14, ...), custom_call_target="tpu_custom_call" | custom-call | bytes 12582912 | tf_op jit(solution)/shard_map/start/pallas_call | solution.py:414
  14.0 0.0 collective-permute-done.3.right_ref
  14.0 0.0 collective-permute-done.2.left_ref
  14.0 0.0 collective-permute-done.1.above_ref
  14.0 1.2 %collective-permute-done.below_ref = f32[240,128]{1,0:T(8,128)S(1)} collective-permute-done((f32[240,128]{1,0:T(8,128)}, f32[240,128]{1,0:T(8,128)S(1)}, u32[]{:S(2)}, u32[]{:S(2)}) %collective-permute-start) | collective-permute-done | bytes 122912 | tf_op jit(solution)/shard_map/ppermute | solution.py:405
  15.2 0.7 solve.2
  15.9 38.9 %all_gather.3.all_maps_ref.all_values_ref = f32[1408,128]{1,0:T(8,128)S(1)} all-gather(f32[88,128]{1,0:T(8,128)S(1)} %get-tuple-element.32), channel_id=1, replica_groups=mesh['normal'=16,'span'=8,'stream'=4] {'normal'}, dimensions={0}, use_global_device_ids=true | all-gather | bytes 765952 | tf_op jit(solution)/shard_map/all_gather | solution.py:434
  54.9 0.7 finish.2.x_ref.refs_0_
  55.6 1.9 %collective-permute-start.7 = (f32[240,128]{1,0:T(8,128)S(1)}, f32[240,128]{1,0:T(8,128)S(1)}, u32[]{:S(2)}, u32[]{:S(2)}) collective-permute-start(f32[240,128]{1,0:T(8,128)S(1)} %finish.2.x_ref.refs_0_), channel_id=1, source_target_pairs={{0,3},{1,0},{2,1},{3,2},{4,7},{5,4},{6,5},{7,6},{8,11},{9,8},{10,9... | collective-permute-start | bytes 368648 | tf_op jit(solution)/shard_map/ppermute | solution.py:405
  57.5 5.1 %collective-permute-start.6 = (f32[240,128]{1,0:T(8,128)S(1)}, f32[240,128]{1,0:T(8,128)S(1)}, u32[]{:S(2)}, u32[]{:S(2)}) collective-permute-start(f32[240,128]{1,0:T(8,128)S(1)} %finish.2.x_ref.refs_0_), channel_id=1, source_target_pairs={{0,1},{1,2},{2,3},{3,0},{4,5},{5,6},{6,7},{7,4},{8,9},{9,10},{10,1... | collective-permute-start | bytes 368648 | tf_op jit(solution)/shard_map/ppermute | solution.py:405
  62.6 0.0 collective-permute-start.5
  62.7 0.5 collective-permute-start.4
  63.2 1.6 %donate.1.refs_11_ = f32[240,128]{1,0:T(8,128)S(1)} custom-call(f32[240,128]{1,0:T(8,128)S(1)} %finish.2.x_ref.refs_0_, s32[48,128]{1,0:T(8,128)S(1)} %get-tuple-element.35.donor_ref), custom_call_target="tpu_custom_call" | custom-call | bytes 6000000 | tf_op jit(solution)/shard_map/donate/pallas_call | solution.py:376
  64.8 0.0 collective-permute-done.7.refs_4_
  64.8 0.3 collective-permute-done.6.refs_3_
  65.1 0.0 collective-permute-done.5.refs_2_
  65.1 3.1 %collective-permute-done.4.refs_1_ = f32[240,128]{1,0:T(8,128)S(1)} collective-permute-done((f32[240,128]{1,0:T(8,128)S(1)}, f32[240,128]{1,0:T(8,128)S(1)}, u32[]{:S(2)}, u32[]{:S(2)}) %collective-permute-start.4) | collective-permute-done | bytes 122912 | tf_op jit(solution)/shard_map/ppermute | solution.py:405
  68.2 0.8 solve.3
  69.0 19.3 %all_to_all.5 = f32[16,10,1,128]{3,2,1,0:T(1,128)S(1)} all-to-all(f32[16,10,1,128]{3,2,1,0:T(1,128)S(1)} %bitcast.12), channel_id=1, replica_groups=mesh['normal'=16,'span'=8,'stream'=4] {'normal'}, dimensions={0} | all-to-all | bytes 163840 | tf_op jit(solution)/shard_map/all_to_all | solution.py:454
  88.3 1.4 %finish.3 = f32[240,128]{1,0:T(8,128)} custom-call(f32[1408,128]{1,0:T(8,128)S(1)} %all_gather.3.all_maps_ref.all_values_ref, f32[160,128]{1,0:T(8,128)S(1)} %bitcast.11, f32[1200,128]{1,0:T(8,128)S(1)} %get-tuple-element.25.lower_ref.refs_7_, f32[1200,128]{1,0:T(8,128)S(1)} %get-tuple-element.26.upper_ref.refs_8_, ...), custom_call_target="tpu_custom_call" | custom-call | bytes 6000000 | tf_op jit(solution)/shard_map/finish/pallas_call | solution.py:376
Async XLA Ops:
  0.0 14.0 %collective-permute-start.3 = (f32[240,128]{1,0:T(8,128)}, f32[240,128]{1,0:T(8,128)S(1)}, u32[]{:S(2)}, u32[]{:S(2)}) collective-permute-start(f32[240,128]{1,0:T(8,128)} %bitcast.18), channel_id=1, source_target_pairs={{0,3},{1,0},{2,1},{3,2},{4,7},{5,4},{6,5},{7,6},{8,11},{9,8},{10,9... | collective-permute-start | bytes 368648 | tf_op jit(solution)/shard_map/ppermute | solution.py:405
  2.6 11.4 %collective-permute-start.2 = (f32[240,128]{1,0:T(8,128)}, f32[240,128]{1,0:T(8,128)S(1)}, u32[]{:S(2)}, u32[]{:S(2)}) collective-permute-start(f32[240,128]{1,0:T(8,128)} %bitcast.19), channel_id=1, source_target_pairs={{0,1},{1,2},{2,3},{3,0},{4,5},{5,6},{6,7},{7,4},{8,9},{9,10},{10,1... | collective-permute-start | bytes 368648 | tf_op jit(solution)/shard_map/ppermute | solution.py:405
  9.4 4.6 %collective-permute-start.1 = (f32[240,128]{1,0:T(8,128)}, f32[240,128]{1,0:T(8,128)S(1)}, u32[]{:S(2)}, u32[]{:S(2)}) collective-permute-start(f32[240,128]{1,0:T(8,128)} %bitcast.20), channel_id=1, source_target_pairs={{0,28},{4,0},{8,4},{12,8},{16,12},{20,16},{24,20},{28,24},{1,29},{... | collective-permute-start | bytes 368648 | tf_op jit(solution)/shard_map/ppermute | solution.py:405
  9.5 5.7 %collective-permute-start = (f32[240,128]{1,0:T(8,128)}, f32[240,128]{1,0:T(8,128)S(1)}, u32[]{:S(2)}, u32[]{:S(2)}) collective-permute-start(f32[240,128]{1,0:T(8,128)} %bitcast.21), channel_id=1, source_target_pairs={{0,4},{4,8},{8,12},{12,16},{16,20},{20,24},{24,28},{28,0},{1,5},{5... | collective-permute-start | bytes 368648 | tf_op jit(solution)/shard_map/ppermute | solution.py:405
  55.6 9.2 %collective-permute-start.7 = (f32[240,128]{1,0:T(8,128)S(1)}, f32[240,128]{1,0:T(8,128)S(1)}, u32[]{:S(2)}, u32[]{:S(2)}) collective-permute-start(f32[240,128]{1,0:T(8,128)S(1)} %finish.2.x_ref.refs_0_), channel_id=1, source_target_pairs={{0,3},{1,0},{2,1},{3,2},{4,7},{5,4},{6,5},{7,6},{8,11},{9,8},{10,9... | collective-permute-start | bytes 368648 | tf_op jit(solution)/shard_map/ppermute | solution.py:405
  57.5 7.6 %collective-permute-start.6 = (f32[240,128]{1,0:T(8,128)S(1)}, f32[240,128]{1,0:T(8,128)S(1)}, u32[]{:S(2)}, u32[]{:S(2)}) collective-permute-start(f32[240,128]{1,0:T(8,128)S(1)} %finish.2.x_ref.refs_0_), channel_id=1, source_target_pairs={{0,1},{1,2},{2,3},{3,0},{4,5},{5,6},{6,7},{7,4},{8,9},{9,10},{10,1... | collective-permute-start | bytes 368648 | tf_op jit(solution)/shard_map/ppermute | solution.py:405
  62.6 2.5 %collective-permute-start.5 = (f32[240,128]{1,0:T(8,128)S(1)}, f32[240,128]{1,0:T(8,128)S(1)}, u32[]{:S(2)}, u32[]{:S(2)}) collective-permute-start(f32[240,128]{1,0:T(8,128)S(1)} %finish.2.x_ref.refs_0_), channel_id=1, source_target_pairs={{0,28},{4,0},{8,4},{12,8},{16,12},{20,16},{24,20},{28,24},{1,29},{... | collective-permute-start | bytes 368648 | tf_op jit(solution)/shard_map/ppermute | solution.py:405
  62.7 5.5 %collective-permute-start.4 = (f32[240,128]{1,0:T(8,128)S(1)}, f32[240,128]{1,0:T(8,128)S(1)}, u32[]{:S(2)}, u32[]{:S(2)}) collective-permute-start(f32[240,128]{1,0:T(8,128)S(1)} %finish.2.x_ref.refs_0_), channel_id=1, source_target_pairs={{0,4},{4,8},{8,12},{12,16},{16,20},{20,24},{24,28},{28,0},{1,5},{5... | collective-permute-start | bytes 368648 | tf_op jit(solution)/shard_map/ppermute | solution.py:405

commit v2 on v1

--- a/solution.py
+++ b/solution.py
@@ -18,7 +18,10 @@
 MAPS = 10
 ROWS = 3 * BLOCK
 VALUES = 2 * COMP
-PADDED = 88
+MEMBERS = 4
+PADDED = 76
+SHARE = PADDED // MEMBERS
+SLOT = VALUES + SHARE
 VMEM = pl.BlockSpec(memory_space=pltpu.VMEM)
 
 
@@ -111,9 +114,25 @@
     donate(x_ref, donor_ref, donated_ref)
 
 
+def summary_kernel(lower_in, upper_in, whole_out, lower_ref, upper_ref, maps_ref, whole_ref, local_ref, moves):
+    copies = [
+        pltpu.make_async_copy(a, b, moves.at[k])
+        for k, (a, b) in enumerate(((lower_in, lower_ref), (upper_in, upper_ref)))
+    ]
+    for copy in copies:
+        copy.start()
+    for copy in copies:
+        copy.wait()
+    make_maps(lower_ref, upper_ref, maps_ref, whole_ref, local_ref)
+    copy = pltpu.make_async_copy(whole_ref, whole_out, moves.at[2])
+    copy.start()
+    copy.wait()
+
+
 def start_kernel(*refs):
-    given, kept = refs[:8], refs[8:16]
-    donated_ref, maps_ref, whole_ref, local_ref, arrived = refs[16:]
+    members_ref, given, kept = refs[0], refs[1:9], refs[9:17]
+    donated_ref, maps_ref, share_ref, outer_ref = refs[17:21]
+    whole_ref, local_ref, group_ref, work_ref, arrived = refs[21:]
     copies = [
         pltpu.make_async_copy(a, b, arrived.at[k]) for k, (a, b) in enumerate(zip(given, kept))
     ]
@@ -123,11 +142,17 @@
     for copy in copies[:2]:
         copy.wait()
     make_maps(lower_ref, upper_ref, maps_ref, whole_ref, local_ref)
+    group_maps(members_ref, share_ref, outer_ref, group_ref, work_ref)
     for copy in copies[2:4]:
         copy.wait()
     donate(x_ref, donor_ref, donated_ref)
     for copy in copies[4:]:
         copy.wait()
+
+
+def put_whole(ref, at, row):
+    for member in range(MEMBERS):
+        ref[pl.ds(member * PADDED + at, 1), :] = row
 
 
 def make_maps(lower_ref, upper_ref, maps_ref, whole_ref, local_ref):
@@ -177,7 +202,7 @@
     put_map(maps_ref, HEAD, head)
     for c in SIZES:
         for e in SIZES:
-            whole_ref[pl.ds(c * COMP + e, 1), :] = window[c][e][PIECES - 1 :, :]
+            put_whole(whole_ref, c * COMP + e, window[c][e][PIECES - 1 :, :])
 
     window = behind
     response = product(fold, head)
@@ -198,12 +223,13 @@
     for c in SIZES:
         for e in SIZES:
             at = c * COMP + e
-            whole_ref[pl.ds(BLOCK + at, 1), :] = response[c][e][:1, :]
-            whole_ref[pl.ds(2 * BLOCK + at, 1), :] = window[c][e][:1, :]
+            put_whole(whole_ref, BLOCK + at, response[c][e][:1, :])
+            put_whole(whole_ref, 2 * BLOCK + at, window[c][e][:1, :])
+    put_whole(whole_ref, ROWS, jnp.zeros((1, LANES), jnp.float32))
 
 
 def solve_kernel(
-    copies,
+    count,
     x_ref,
     below_ref,
     above_ref,
@@ -217,7 +243,8 @@
     iblank_ref,
     donated_ref,
     maps_ref,
-    whole_ref,
+    outer_ref,
+    share_ref,
     sent_ref,
     scaled_ref,
     starts_ref,
@@ -276,31 +303,89 @@
     put_packed(
         starts_ref, 1, [jnp.where(piece == PIECES - 1, 0.0, moved(a, -1)) for a in behind]
     )
-    if whole_ref is not None:
-        sent_ref[pl.ds(0, ROWS), :] = whole_ref[...]
-        base = ROWS
-        sent_ref[pl.ds(ROWS + VALUES, PADDED - ROWS - VALUES), :] = jnp.zeros(
-            (PADDED - ROWS - VALUES, LANES), jnp.float32
-        )
-    else:
-        base = 0
-    for copy in range(copies):
-        for c in SIZES:
-            at = base + copy * VALUES + c
-            sent_ref[pl.ds(at, 1), :] = ahead[c][PIECES - 1 :, :]
-            sent_ref[pl.ds(at + COMP, 1), :] = behind[c][:1, :]
-
-
-def solve_without(copies, *refs):
-    solve_kernel(copies, *refs[:13], None, *refs[13:])
+    y_out = [jnp.broadcast_to(a[PIECES - 1 :, :], (COMP, LANES)) for a in ahead]
+    x_out = [jnp.broadcast_to(a[:1, :], (COMP, LANES)) for a in behind]
+    row = lax.broadcasted_iota(jnp.int32, (COMP, LANES), 0)
+
+    def stacked(rows):
+        out = rows[0]
+        for c in SIZES[1:]:
+            out = jnp.where(row == c, rows[c], out)
+        return out
+
+    def outer(which, rows):
+        return total([outer_ref[pl.ds((which * COMP + e) * PIECES, COMP), :] * rows[e] for e in SIZES])
+
+    inside = stacked(y_out), stacked(x_out)
+    outside = outer(0, y_out), outer(1, y_out) + outer(2, x_out)
+    mine = lax.axis_index("normal") // MEMBERS
+    slot = VALUES if share_ref is None else SLOT
+    for device in range(count):
+        same = mine == device // MEMBERS
+        for k in range(2):
+            at = device * slot + k * COMP
+            sent_ref[pl.ds(at, COMP), :] = jnp.where(same, inside[k], outside[k])
+        if share_ref is not None:
+            sent_ref[pl.ds(device * slot + VALUES, SHARE), :] = share_ref[pl.ds(0, SHARE), :]
+
+
+def solve_without(count, *refs):
+    solve_kernel(count, *refs[:14], None, *refs[14:])
+
+
+def group_maps(members_ref, share_ref, outer_ref, whole_ref, work_ref):
+    own = lax.rem(lax.axis_index("normal"), MEMBERS)
+    row = lax.broadcasted_iota(jnp.int32, (COMP, LANES), 0)
+    eye = [jnp.where(row == e, 1.0, 0.0) for e in SIZES]
+    none = [jnp.zeros((COMP, LANES), jnp.float32)] * COMP
+
+    def given(member, which):
+        base = member * PADDED + which * BLOCK
+        columns = [members_ref[pl.ds(base + e, COMP, stride=COMP), :] for e in SIZES]
+        return columns, lambda k, e: members_ref[pl.ds(base + k * COMP + e, 1), :]
+
+    def kept(columns, place):
+        for e in SIZES:
+            work_ref[pl.ds((place * COMP + e) * PIECES, COMP), :] = columns[e]
+        return lambda k, e: work_ref[pl.ds((place * COMP + e) * PIECES + k, 1), :]
+
+    def multiply(columns, element):
+        return [total([columns[k] * element(k, e) for k in SIZES]) for e in SIZES]
+
+    def chosen(options):
+        out = options[-1]
+        for member in range(MEMBERS - 1):
+            out = [jnp.where(own == member, a, b) for a, b in zip(options[member], out)]
+        return out
+
+    onward, across = [given(MEMBERS - 1, 0)[0]], [given(MEMBERS - 1, 1)[0]]
+    for member in range(MEMBERS - 2, -1, -1):
+        forward = given(member, 0)[1]
+        onward.insert(0, multiply(onward[0], forward))
+        inner = kept(multiply(across[0], forward), member)
+        across.insert(0, add(given(member, 1)[0], multiply(given(member, 2)[0], inner)))
+    back = [eye, given(0, 2)[0]]
+    for member in range(1, MEMBERS):
+        back.append(multiply(back[-1], given(member, 2)[1]))
+    mixed = multiply(
+        chosen(back[1:MEMBERS] + [none]), kept(chosen(across[1:] + [none]), MEMBERS - 1)
+    )
+    for k, columns in enumerate((chosen(onward[1:] + [eye]), mixed, chosen(back[:MEMBERS]))):
+        for e in SIZES:
+            outer_ref[pl.ds((k * COMP + e) * PIECES, COMP), :] = columns[e]
+    for k, columns in enumerate((onward[0], across[0], back[MEMBERS])):
+        for e in SIZES:
+            whole_ref[pl.ds(k * BLOCK + e, COMP, stride=COMP), :] = columns[e]
+    whole_ref[pl.ds(ROWS, 1), :] = jnp.zeros((1, LANES), jnp.float32)
+    share_ref[pl.ds(0, SHARE), :] = whole_ref[pl.ds(own * SHARE, SHARE), :]
 
 
 def finish_kernel(
     count,
-    stride,
-    offset,
-    all_maps_ref,
-    all_values_ref,
+    slot,
+    values_ref,
+    shares_ref,
+    members_ref,
     lower_ref,
     upper_ref,
     maps_ref,
@@ -311,35 +396,63 @@
     entry_ref,
 ):
     me = lax.axis_index("normal")
-
-    def row_map(base):
-        return [[all_maps_ref[pl.ds(base + c * COMP + e, 1), :] for e in SIZES] for c in SIZES]
-
-    def row_vector(base):
-        return [all_values_ref[pl.ds(base + c, 1), :] for c in SIZES]
+    mine, own = me // MEMBERS, lax.rem(me, MEMBERS)
+    groups = count // MEMBERS
+
+    def group_map(group, which):
+        def row(at):
+            place = (group * MEMBERS + at // SHARE) * SLOT + VALUES + at % SHARE
+            return shares_ref[pl.ds(place, 1), :]
+
+        return [[row((which * COMP + c) * COMP + e) for e in SIZES] for c in SIZES]
+
+    def member_map(member, which):
+        base = member * PADDED + which * BLOCK
+        return [[members_ref[pl.ds(base + c * COMP + e, 1), :] for e in SIZES] for c in SIZES]
+
+    def value(device, which):
+        return [values_ref[pl.ds(device * slot + which * COMP + c, 1), :] for c in SIZES]
+
+    def group_value(group, which):
+        parts = [value(group * MEMBERS + member, which) for member in range(MEMBERS)]
+        return [total([part[c] for part in parts]) for c in SIZES]
+
+    def put_entry(at, state):
+        for c in SIZES:
+            entry_ref[pl.ds(at * PIECES + c, 1), :] = state[c]
+
+    def entry(at):
+        return [entry_ref[pl.ds(at * PIECES + c, 1), :] for c in SIZES]
 
     none = (jnp.zeros((1, LANES), jnp.float32),) * COMP
 
-    def forward(device, state):
-        for c in SIZES:
-            entry_ref[pl.ds(device * PIECES + c, 1), :] = state[c]
-        value = row_vector(device * stride + offset)
-        return tuple(add(value, times(row_map(device * PADDED), list(state))))
-
-    lax.fori_loop(0, count, forward, none)
-
-    def state_of(device):
-        return [entry_ref[pl.ds(device * PIECES + c, 1), :] for c in SIZES]
-
-    def backward(step, state):
-        device = count - 1 - step
-        value = row_vector(device * stride + offset + COMP)
-        value = add(value, times(row_map(device * PADDED + BLOCK), state_of(device)))
-        return tuple(add(value, times(row_map(device * PADDED + 2 * BLOCK), list(state))))
-
-    x_in = lax.fori_loop(0, count - 1 - me, backward, none)
-
-    y_in = [jnp.broadcast_to(a, (PIECES, LANES)) for a in state_of(me)]
+    def over_group(group, state):
+        put_entry(group, state)
+        return tuple(add(group_value(group, 0), times(group_map(group, 0), list(state))))
+
+    state = lax.fori_loop(0, mine, over_group, none)
+    for member in range(MEMBERS):
+        put_entry(groups + member, state)
+        state = add(value(mine * MEMBERS + member, 0), times(member_map(member, 0), list(state)))
+    lax.fori_loop(mine + 1, groups, over_group, tuple(state))
+
+    def back_over_group(step, state):
+        group = groups - 1 - step
+        inner = add(group_value(group, 1), times(group_map(group, 1), entry(group)))
+        return tuple(add(inner, times(group_map(group, 2), list(state))))
+
+    state = lax.fori_loop(0, groups - 1 - mine, back_over_group, none)
+
+    def back_over_member(step, state):
+        member = MEMBERS - 1 - step
+        inner = add(
+            value(mine * MEMBERS + member, 1), times(member_map(member, 1), entry(groups + member))
+        )
+        return tuple(add(inner, times(member_map(member, 2), list(state))))
+
+    x_in = lax.fori_loop(0, MEMBERS - 1 - own, back_over_member, state)
+
+    y_in = [jnp.broadcast_to(a, (PIECES, LANES)) for a in entry(groups + own)]
     x_in = [jnp.broadcast_to(a, (PIECES, LANES)) for a in x_in]
 
     y_start = add(packed_at(starts_ref, 0), times(map_at(maps_ref, HEAD), y_in))
@@ -371,15 +484,21 @@
     return pltpu.VMEM((rows, LANES), jnp.float32)
 
 
-def call(kernel, inputs, out_rows, scratch_rows, name, micros, limit=16 << 20):
-    out_shape = [floats(r) for r in out_rows]
+def call(kernel, inputs, outputs, scratches, name, micros, far=()):
+    hbm = pl.BlockSpec(memory_space=pltpu.HBM)
+    places = range(len(inputs) + len(outputs))
+    specs = [hbm if k in far else VMEM for k in places]
+    inputs = [
+        pltpu.with_memory_space_constraint(a, pltpu.HBM) if k in far else a
+        for k, a in enumerate(inputs)
+    ]
     return pl.pallas_call(
         kernel,
-        out_shape=out_shape,
-        in_specs=[VMEM] * len(inputs),
-        out_specs=[VMEM] * len(out_rows),
-        scratch_shapes=[scratch(r) for r in scratch_rows],
-        compiler_params=pltpu.CompilerParams(vmem_limit_bytes=limit),
+        out_shape=[floats(a) if isinstance(a, int) else a for a in outputs],
+        in_specs=specs[: len(inputs)],
+        out_specs=specs[len(inputs) :],
+        scratch_shapes=[scratch(a) if isinstance(a, int) else a for a in scratches],
+        compiler_params=pltpu.CompilerParams(vmem_limit_bytes=16 << 20),
         cost_estimate=pl.CostEstimate(
             flops=0, bytes_accessed=int(micros * 3.0e6), transcendentals=0
         ),
@@ -407,58 +526,89 @@
             for step in (1, -1)
         ]
 
+    def exchanged(rows, parts, groups=None):
+        rows = rows.reshape(parts, -1, 1, LANES)
+        return lax.all_to_all(rows, "normal", 0, 0, axis_index_groups=groups).reshape(-1, LANES)
+
+    maps_rows = MAPS * BLOCK * PIECES
+    local_rows = STEPS * BLOCK * PIECES
+    whole_rows = MEMBERS * PADDED
+    entries = (count // MEMBERS + MEMBERS) * PIECES
+
+    (whole,) = call(
+        summary_kernel,
+        (lower, upper),
+        (whole_rows,),
+        (
+            lower.shape[0],
+            upper.shape[0],
+            maps_rows,
+            whole_rows,
+            local_rows,
+            pltpu.SemaphoreType.DMA((3,)),
+        ),
+        "summary",
+        2,
+        far=(0, 1, 2),
+    )
+    groups = [list(range(k, k + MEMBERS)) for k in range(0, count, MEMBERS)]
+    members = exchanged(whole, MEMBERS, groups)
     near = around(x)
     given = (lower, upper, x, donor, source, pivot, coupling, iblank)
-    shapes = [jax.ShapeDtypeStruct(a.shape, a.dtype) for a in given]
-    shapes += [floats(r) for r in (state, MAPS * BLOCK * PIECES, ROWS)]
-    *given, donated, maps, whole = pl.pallas_call(
+    *given, donated, maps, share, outer = call(
         start_kernel,
-        out_shape=shapes,
-        in_specs=[pl.BlockSpec(memory_space=pltpu.HBM)] * len(given),
-        out_specs=[VMEM] * len(shapes),
-        scratch_shapes=[scratch(STEPS * BLOCK * PIECES), pltpu.SemaphoreType.DMA((len(given),))],
-        compiler_params=pltpu.CompilerParams(vmem_limit_bytes=16 << 20),
-        cost_estimate=pl.CostEstimate(flops=0, bytes_accessed=12 << 20, transcendentals=0),
-        name="start",
-    )(*(pltpu.with_memory_space_constraint(a, pltpu.HBM) for a in given))
+        (members, *given),
+        [jax.ShapeDtypeStruct(a.shape, a.dtype) for a in given]
+        + [state, maps_rows, 24, 3 * COMP * PIECES],
+        (
+            whole_rows,
+            local_rows,
+            PADDED + 4,
+            MEMBERS * COMP * PIECES,
+            pltpu.SemaphoreType.DMA((len(given),)),
+        ),
+        "start",
+        4,
+        far=range(1, len(given) + 1),
+    )
     lower, upper, x, donor, source, pivot, coupling, iblank = given
     fixed = (source, pivot, lower, upper, coupling, iblank)
     sent, scaled, starts = call(
-        functools.partial(solve_kernel, 1),
-        (x, *near, *fixed, donated, maps, whole),
-        (PADDED, state, 2 * COMP * PIECES),
+        functools.partial(solve_kernel, count),
+        (x, *near, *fixed, donated, maps, outer, share),
+        (count * SLOT, state, 2 * COMP * PIECES),
         (state,),
         "solve",
         2,
     )
-    everyone = lax.all_gather(sent, "normal", tiled=True)
+    shares = exchanged(sent, count)
     (x,) = call(
-        functools.partial(finish_kernel, count, PADDED, ROWS),
-        (everyone, everyone, lower, upper, maps, scaled, starts),
+        functools.partial(finish_kernel, count, SLOT),
+        (shares, shares, members, lower, upper, maps, scaled, starts),
         (field,),
-        (state, count * PIECES),
+        (state, entries),
         "finish",
-        2,
+        1,
     )
 
     near = around(x)
     (donated,) = call(donate_kernel, (x, donor), (state,), (), "donate", 2)
     sent, scaled, starts = call(
         functools.partial(solve_without, count),
-        (x, *near, *fixed, donated, maps),
+        (x, *near, *fixed, donated, maps, outer),
         (count * VALUES, state, 2 * COMP * PIECES),
         (state,),
         "solve",
         2,
     )
-    values = lax.all_to_all(sent.reshape(count, VALUES, 1, LANES), "normal", 0, 0)
+    values = exchanged(sent, count)
     (x,) = call(
-        functools.partial(finish_kernel, count, VALUES, 0),
-        (everyone, values.reshape(-1, LANES), lower, upper, maps, scaled, starts),
+        functools.partial(finish_kernel, count, VALUES),
+        (values, shares, members, lower, upper, maps, scaled, starts),
         (field,),
-        (state, count * PIECES),
+        (state, entries),
         "finish",
-        2,
+        1,
     )
     return x.reshape(iterate.shape)
 

time: 89.9 us -> 88.6 us (0.986)
  blocking collectives: 58.2 us -> 49.6 us
  starting transfers between devices: 17.5 us -> 21.9 us
  Pallas kernels: 9.23 us -> 11.7 us
    all_gather x1 -> x0, blocking collectives: 38.9 us -> none  [per_device(): everyone = lax.all_gather(sent, 'normal', tiled=True)]
    all_to_all x1 -> x2, blocking collectives: 19.3 us -> 49.6 us  [exchanged(): lax.all_to_all(rows, 'normal', 0, 0, axis_index_groups=groups)]
    all_to_all x0 -> x1, starting transfers between devices: none -> 5.91 us  [exchanged(): lax.all_to_all(rows, 'normal', 0, 0, axis_index_groups=groups)]
    pallas_call x6 -> x7, Pallas kernels: 9.23 us -> 11.7 us  [call(): pl.pallas_call(kernel, out_shape=[floats(a) if isinstance(a, int) else a...]
    ppermute x8, starting transfers between devices: 17.5 us -> 16 us  [around(): lax.ppermute(x, axis, ring(lax.axis_size(axis), step))]
  transfers between devices with their start and end apart: 8 -> 9, of which waited for: 3 -> 3; matrix products, arithmetic and copies ran while one was open for 0% -> 0% of each run, Pallas kernels for 6% -> 6%
where the time goes in v2:
time: 88.6 us; the launch traced here: 88.3 us
  blocking collectives  49.6 us (56%)
  starting transfers between devices  21.9 us (25%)
  Pallas kernels  11.7 us (13%)
  waiting for transfers between devices  4.97 us (6%)
    all_to_all x2, blocking collectives, exchanged(): lax.all_to_all(rows, 'normal', 0, 0, axis_index_groups=groups)  49.6 us
    ppermute x8, starting transfers between devices, around(): lax.ppermute(x, axis, ring(lax.axis_size(axis), step))  16 us
    pallas_call x7, Pallas kernels, call(): pl.pallas_call(kernel, out_shape=[floats(a) if isinstance(a, int) else a...  11.7 us
    all_to_all x1, starting transfers between devices, exchanged(): lax.all_to_all(rows, 'normal', 0, 0, axis_index_groups=groups)  5.91 us
    ppermute x8, waiting for transfers between devices, around(): lax.ppermute(x, axis, ring(lax.axis_size(axis), step))  4.97 us
  transfers between devices with their start and end apart: 9, of which 3 were waited for; matrix products, arithmetic and copies ran while one was open for 0% of the time, Pallas kernels for 6%

profile of v2, /device:TPU:24, one launch (start us, length us, event | category | flops | bytes accessed | tf_op | source)
XLA Modules:
  0.0 88.3 jit_solution(2600229398879394571)
XLA Ops:
  0.0 3.0 %summary.1 = f32[304,128]{1,0:T(8,128)} custom-call(f32[1200,128]{1,0:T(8,128)} %bitcast.25, f32[1200,128]{1,0:T(8,128)} %bitcast.27), custom_call_target="tpu_custom_call" | custom-call | bytes 6000000 | tf_op jit(solution)/shard_map/summary/pallas_call | solution.py:495
  3.0 5.9 %all-to-all-start = ((f32[4,76,1,128]{3,2,1,0:T(1,128)}), f32[4,76,1,128]{3,2,1,0:T(1,128)S(1)}, u32[]{:S(2)}, u32[]{:S(2)}) async-start(f32[4,76,1,128]{3,2,1,0:T(1,128)} %bitcast.2), calls=%async_computation | async-start | bytes 311296 | tf_op jit(solution)/shard_map/all_to_all | solution.py:531
  8.9 2.6 %collective-permute-start.3 = (f32[240,128]{1,0:T(8,128)}, f32[240,128]{1,0:T(8,128)S(1)}, u32[]{:S(2)}, u32[]{:S(2)}) collective-permute-start(f32[240,128]{1,0:T(8,128)} %bitcast.31), channel_id=1, source_target_pairs={{0,3},{1,0},{2,1},{3,2},{4,7},{5,4},{6,5},{7,6},{8,11},{9,8},{10,9... | collective-permute-start | bytes 368648 | tf_op jit(solution)/shard_map/ppermute | solution.py:524
  11.5 4.4 %collective-permute-start.2 = (f32[240,128]{1,0:T(8,128)}, f32[240,128]{1,0:T(8,128)S(1)}, u32[]{:S(2)}, u32[]{:S(2)}) collective-permute-start(f32[240,128]{1,0:T(8,128)} %bitcast.32), channel_id=1, source_target_pairs={{0,1},{1,2},{2,3},{3,0},{4,5},{5,6},{6,7},{7,4},{8,9},{9,10},{10,1... | collective-permute-start | bytes 368648 | tf_op jit(solution)/shard_map/ppermute | solution.py:524
  15.9 1.4 %collective-permute-start.1 = (f32[240,128]{1,0:T(8,128)}, f32[240,128]{1,0:T(8,128)S(1)}, u32[]{:S(2)}, u32[]{:S(2)}) collective-permute-start(f32[240,128]{1,0:T(8,128)} %bitcast.33), channel_id=1, source_target_pairs={{0,28},{4,0},{8,4},{12,8},{16,12},{20,16},{24,20},{28,24},{1,29},{... | collective-permute-start | bytes 368648 | tf_op jit(solution)/shard_map/ppermute | solution.py:524
  17.3 0.0 collective-permute-start
  17.3 0.0 all-to-all-done
  17.3 4.1 %start.1 = (f32[1200,128]{1,0:T(8,128)S(1)}, f32[1200,128]{1,0:T(8,128)S(1)}, f32[240,128]{1,0:T(8,128)S(1)}, s32[48,128]{1,0:T(8,128)S(1)}, f32[240,128]{1,0:T(...) custom-call(f32[304,128]{1,0:T(8,128)S(1)} %bitcast.18, ...), custom_call_target="tpu_custom_call" | custom-call | bytes 12000000 | tf_op jit(solution)/shard_map/start/pallas_call | solution.py:495
  21.4 0.0 collective-permute-done.3.right_ref
  21.4 0.0 collective-permute-done.2.left_ref
  21.4 0.0 collective-permute-done.1.above_ref
  21.4 1.6 %collective-permute-done.below_ref = f32[240,128]{1,0:T(8,128)S(1)} collective-permute-done((f32[240,128]{1,0:T(8,128)}, f32[240,128]{1,0:T(8,128)S(1)}, u32[]{:S(2)}, u32[]{:S(2)}) %collective-permute-start) | collective-permute-done | bytes 122912 | tf_op jit(solution)/shard_map/ppermute | solution.py:524
  23.0 0.8 solve.2
  23.8 29.9 %all_to_all.15 = f32[16,29,1,128]{3,2,1,0:T(1,128)S(1)} all-to-all(f32[16,29,1,128]{3,2,1,0:T(1,128)S(1)} %bitcast.22), channel_id=1, replica_groups=mesh['normal'=16,'span'=8,'stream'=4] {'normal'}, dimensions={0} | all-to-all | bytes 475136 | tf_op jit(solution)/shard_map/all_to_all | solution.py:531
  53.7 0.4 finish.2.x_ref.refs_0_
  54.1 1.9 %collective-permute-start.7 = (f32[240,128]{1,0:T(8,128)S(1)}, f32[240,128]{1,0:T(8,128)S(1)}, u32[]{:S(2)}, u32[]{:S(2)}) collective-permute-start(f32[240,128]{1,0:T(8,128)S(1)} %finish.2.x_ref.refs_0_), channel_id=1, source_target_pairs={{0,3},{1,0},{2,1},{3,2},{4,7},{5,4},{6,5},{7,6},{8,11},{9,8},{10,9... | collective-permute-start | bytes 368648 | tf_op jit(solution)/shard_map/ppermute | solution.py:524
  56.0 5.1 %collective-permute-start.6 = (f32[240,128]{1,0:T(8,128)S(1)}, f32[240,128]{1,0:T(8,128)S(1)}, u32[]{:S(2)}, u32[]{:S(2)}) collective-permute-start(f32[240,128]{1,0:T(8,128)S(1)} %finish.2.x_ref.refs_0_), channel_id=1, source_target_pairs={{0,1},{1,2},{2,3},{3,0},{4,5},{5,6},{6,7},{7,4},{8,9},{9,10},{10,1... | collective-permute-start | bytes 368648 | tf_op jit(solution)/shard_map/ppermute | solution.py:524
  61.2 0.0 collective-permute-start.5
  61.2 0.5 collective-permute-start.4
  61.7 1.6 %donate.1.refs_11_ = f32[240,128]{1,0:T(8,128)S(1)} custom-call(f32[240,128]{1,0:T(8,128)S(1)} %finish.2.x_ref.refs_0_, s32[48,128]{1,0:T(8,128)S(1)} %get-tuple-element.37.donor_ref), custom_call_target="tpu_custom_call" | custom-call | bytes 6000000 | tf_op jit(solution)/shard_map/donate/pallas_call | solution.py:495
  63.4 0.0 collective-permute-done.7.refs_4_
  63.4 0.2 collective-permute-done.6.refs_3_
  63.6 0.0 collective-permute-done.5.refs_2_
  63.6 3.1 %collective-permute-done.4.refs_1_ = f32[240,128]{1,0:T(8,128)S(1)} collective-permute-done((f32[240,128]{1,0:T(8,128)S(1)}, f32[240,128]{1,0:T(8,128)S(1)}, u32[]{:S(2)}, u32[]{:S(2)}) %collective-permute-start.4) | collective-permute-done | bytes 122912 | tf_op jit(solution)/shard_map/ppermute | solution.py:524
  66.7 0.8 solve.3
  67.5 19.7 %all_to_all.16 = f32[16,10,1,128]{3,2,1,0:T(1,128)S(1)} all-to-all(f32[16,10,1,128]{3,2,1,0:T(1,128)S(1)} %bitcast.23), channel_id=1, replica_groups=mesh['normal'=16,'span'=8,'stream'=4] {'normal'}, dimensions={0} | all-to-all | bytes 163840 | tf_op jit(solution)/shard_map/all_to_all | solution.py:531
  87.2 1.1 %finish.3 = f32[240,128]{1,0:T(8,128)} custom-call(f32[160,128]{1,0:T(8,128)S(1)} %bitcast.21, f32[464,128]{1,0:T(8,128)S(1)} %bitcast.17, f32[304,128]{1,0:T(8,128)S(1)} %bitcast.20, f32[1200,128]{1,0:T(8,128)S(1)} %get-tuple-element.26.lower_ref.refs_7_, f32[1200,128]{1,0:T(8,128)S(1)} %get-tuple-element.27.upper_ref.refs_8_, ...), custom_call_target="tpu_custom_call" | custom-call | bytes 3000000 | tf_op jit(solution)/shard_map/finish/pallas_call | solution.py:495
Async XLA Ops:
  3.0 14.3 %all-to-all-start = ((f32[4,76,1,128]{3,2,1,0:T(1,128)}), f32[4,76,1,128]{3,2,1,0:T(1,128)S(1)}, u32[]{:S(2)}, u32[]{:S(2)}) async-start(f32[4,76,1,128]{3,2,1,0:T(1,128)} %bitcast.2), calls=%async_computation | async-start | bytes 311296 | tf_op jit(solution)/shard_map/all_to_all | solution.py:531
  8.9 12.5 %collective-permute-start.3 = (f32[240,128]{1,0:T(8,128)}, f32[240,128]{1,0:T(8,128)S(1)}, u32[]{:S(2)}, u32[]{:S(2)}) collective-permute-start(f32[240,128]{1,0:T(8,128)} %bitcast.31), channel_id=1, source_target_pairs={{0,3},{1,0},{2,1},{3,2},{4,7},{5,4},{6,5},{7,6},{8,11},{9,8},{10,9... | collective-permute-start | bytes 368648 | tf_op jit(solution)/shard_map/ppermute | solution.py:524
  11.5 9.9 %collective-permute-start.2 = (f32[240,128]{1,0:T(8,128)}, f32[240,128]{1,0:T(8,128)S(1)}, u32[]{:S(2)}, u32[]{:S(2)}) collective-permute-start(f32[240,128]{1,0:T(8,128)} %bitcast.32), channel_id=1, source_target_pairs={{0,1},{1,2},{2,3},{3,0},{4,5},{5,6},{6,7},{7,4},{8,9},{9,10},{10,1... | collective-permute-start | bytes 368648 | tf_op jit(solution)/shard_map/ppermute | solution.py:524
  15.9 5.5 %collective-permute-start.1 = (f32[240,128]{1,0:T(8,128)}, f32[240,128]{1,0:T(8,128)S(1)}, u32[]{:S(2)}, u32[]{:S(2)}) collective-permute-start(f32[240,128]{1,0:T(8,128)} %bitcast.33), channel_id=1, source_target_pairs={{0,28},{4,0},{8,4},{12,8},{16,12},{20,16},{24,20},{28,24},{1,29},{... | collective-permute-start | bytes 368648 | tf_op jit(solution)/shard_map/ppermute | solution.py:524
  17.3 5.7 %collective-permute-start = (f32[240,128]{1,0:T(8,128)}, f32[240,128]{1,0:T(8,128)S(1)}, u32[]{:S(2)}, u32[]{:S(2)}) collective-permute-start(f32[240,128]{1,0:T(8,128)} %bitcast.34), channel_id=1, source_target_pairs={{0,4},{4,8},{8,12},{12,16},{16,20},{20,24},{24,28},{28,0},{1,5},{5... | collective-permute-start | bytes 368648 | tf_op jit(solution)/shard_map/ppermute | solution.py:524
  54.1 9.2 %collective-permute-start.7 = (f32[240,128]{1,0:T(8,128)S(1)}, f32[240,128]{1,0:T(8,128)S(1)}, u32[]{:S(2)}, u32[]{:S(2)}) collective-permute-start(f32[240,128]{1,0:T(8,128)S(1)} %finish.2.x_ref.refs_0_), channel_id=1, source_target_pairs={{0,3},{1,0},{2,1},{3,2},{4,7},{5,4},{6,5},{7,6},{8,11},{9,8},{10,9... | collective-permute-start | bytes 368648 | tf_op jit(solution)/shard_map/ppermute | solution.py:524
  56.0 7.6 %collective-permute-start.6 = (f32[240,128]{1,0:T(8,128)S(1)}, f32[240,128]{1,0:T(8,128)S(1)}, u32[]{:S(2)}, u32[]{:S(2)}) collective-permute-start(f32[240,128]{1,0:T(8,128)S(1)} %finish.2.x_ref.refs_0_), channel_id=1, source_target_pairs={{0,1},{1,2},{2,3},{3,0},{4,5},{5,6},{6,7},{7,4},{8,9},{9,10},{10,1... | collective-permute-start | bytes 368648 | tf_op jit(solution)/shard_map/ppermute | solution.py:524
  61.2 2.5 %collective-permute-start.5 = (f32[240,128]{1,0:T(8,128)S(1)}, f32[240,128]{1,0:T(8,128)S(1)}, u32[]{:S(2)}, u32[]{:S(2)}) collective-permute-start(f32[240,128]{1,0:T(8,128)S(1)} %finish.2.x_ref.refs_0_), channel_id=1, source_target_pairs={{0,28},{4,0},{8,4},{12,8},{16,12},{20,16},{24,20},{28,24},{1,29},{... | collective-permute-start | bytes 368648 | tf_op jit(solution)/shard_map/ppermute | solution.py:524
  61.2 5.5 %collective-permute-start.4 = (f32[240,128]{1,0:T(8,128)S(1)}, f32[240,128]{1,0:T(8,128)S(1)}, u32[]{:S(2)}, u32[]{:S(2)}) collective-permute-start(f32[240,128]{1,0:T(8,128)S(1)} %finish.2.x_ref.refs_0_), channel_id=1, source_target_pairs={{0,4},{4,8},{8,12},{12,16},{16,20},{20,24},{24,28},{28,0},{1,5},{5... | collective-permute-start | bytes 368648 | tf_op jit(solution)/shard_map/ppermute | solution.py:524

commit v3 on v2

--- a/solution.py
+++ b/solution.py
@@ -114,6 +114,19 @@
     donate(x_ref, donor_ref, donated_ref)
 
 
+def no_edges():
+    return (jnp.zeros((PIECES, LANES), jnp.float32),) * 2
+
+
+def with_edges(vector, step, first, last):
+    lane = lax.broadcasted_iota(jnp.int32, (PIECES, LANES), 1)
+    for c in SIZES:
+        here = lane == step * COMP + c
+        first = jnp.where(here, jnp.broadcast_to(vector[c][:, :1], (PIECES, LANES)), first)
+        last = jnp.where(here, jnp.broadcast_to(vector[c][:, -1:], (PIECES, LANES)), last)
+    return first, last
+
+
 def summary_kernel(lower_in, upper_in, whole_out, lower_ref, upper_ref, maps_ref, whole_ref, local_ref, moves):
     copies = [
         pltpu.make_async_copy(a, b, moves.at[k])
@@ -139,10 +152,10 @@
     for copy in copies:
         copy.start()
     lower_ref, upper_ref, x_ref, donor_ref = kept[:4]
+    group_maps(members_ref, share_ref, outer_ref, group_ref, work_ref)
     for copy in copies[:2]:
         copy.wait()
     make_maps(lower_ref, upper_ref, maps_ref, whole_ref, local_ref)
-    group_maps(members_ref, share_ref, outer_ref, group_ref, work_ref)
     for copy in copies[2:4]:
         copy.wait()
     donate(x_ref, donor_ref, donated_ref)
@@ -256,14 +269,27 @@
 
     def forward(step, state):
         x = vector_at(x_ref, step)
-        before = [
-            pltpu.roll(jnp.where(lane == LANES - 1, a, b), 1, 1)
-            for a, b in zip(vector_at(left_ref, step), x)
-        ]
-        after = [
-            pltpu.roll(jnp.where(lane == 0, a, b), LANES - 1, 1)
-            for a, b in zip(vector_at(right_ref, step), x)
-        ]
+        if left_ref.shape[0] == PIECES:
+            before, after = [], []
+            for c in SIZES:
+                place = jnp.full((PIECES, LANES), step * COMP + c, jnp.int32)
+                for out, edges_ref, turn, at in (
+                    (before, left_ref, 1, 0),
+                    (after, right_ref, LANES - 1, LANES - 1),
+                ):
+                    edge = jnp.take_along_axis(
+                        edges_ref[...], place, axis=1, mode="promise_in_bounds"
+                    )
+                    out.append(jnp.where(lane == at, edge, pltpu.roll(x[c], turn, 1)))
+        else:
+            before = [
+                pltpu.roll(jnp.where(lane == LANES - 1, a, b), 1, 1)
+                for a, b in zip(vector_at(left_ref, step), x)
+            ]
+            after = [
+                pltpu.roll(jnp.where(lane == 0, a, b), LANES - 1, 1)
+                for a, b in zip(vector_at(right_ref, step), x)
+            ]
         near = [vector_at(below_ref, step), vector_at(above_ref, step), before, after]
         rhs = vector_at(source_ref, step)
         for direc in range(4):
@@ -392,6 +418,8 @@
     scaled_ref,
     starts_ref,
     out_ref,
+    first_ref,
+    last_ref,
     states_ref,
     entry_ref,
 ):
@@ -466,14 +494,24 @@
 
     lax.fori_loop(0, STEPS, ahead, tuple(y_start))
 
-    def behind(turn, state):
+    def behind(turn, carry):
+        state, edges = carry
         step = STEPS - 1 - turn
         state = less(packed_at(states_ref, step), times(block_at(upper_ref, step), list(state)))
         for c in SIZES:
             out_ref[pl.ds(step * COMP + c, PIECES, stride=STEPS * COMP), :] = state[c]
-        return tuple(state)
-
-    lax.fori_loop(0, STEPS, behind, tuple(x_start))
+        if first_ref is not None:
+            edges = with_edges(state, step, *edges)
+        return tuple(state), edges
+
+    edges = () if first_ref is None else no_edges()
+    _, edges = lax.fori_loop(0, STEPS, behind, (tuple(x_start), edges))
+    if first_ref is not None:
+        first_ref[...], last_ref[...] = edges
+
+
+def finish_without(count, slot, *refs):
+    finish_kernel(count, slot, *refs[:9], None, None, *refs[9:])
 
 
 def floats(rows):
@@ -519,12 +557,9 @@
     field = POINTS * COMP
     state = STEPS * COMP * PIECES
 
-    def around(x):
-        return [
-            lax.ppermute(x, axis, ring(lax.axis_size(axis), step))
-            for axis in ("span", "stream")
-            for step in (1, -1)
-        ]
+    def both(up, down, axis):
+        size = lax.axis_size(axis)
+        return [lax.ppermute(up, axis, ring(size, 1)), lax.ppermute(down, axis, ring(size, -1))]
 
     def exchanged(rows, parts, groups=None):
         rows = rows.reshape(parts, -1, 1, LANES)
@@ -553,7 +588,7 @@
     )
     groups = [list(range(k, k + MEMBERS)) for k in range(0, count, MEMBERS)]
     members = exchanged(whole, MEMBERS, groups)
-    near = around(x)
+    near = both(x, x, "span") + both(x, x, "stream")
     given = (lower, upper, x, donor, source, pivot, coupling, iblank)
     *given, donated, maps, share, outer = call(
         start_kernel,
@@ -582,16 +617,16 @@
         2,
     )
     shares = exchanged(sent, count)
-    (x,) = call(
+    x, first, last = call(
         functools.partial(finish_kernel, count, SLOT),
         (shares, shares, members, lower, upper, maps, scaled, starts),
-        (field,),
+        (field, PIECES, PIECES),
         (state, entries),
         "finish",
         1,
     )
 
-    near = around(x)
+    near = both(x, x, "span") + both(last, first, "stream")
     (donated,) = call(donate_kernel, (x, donor), (state,), (), "donate", 2)
     sent, scaled, starts = call(
         functools.partial(solve_without, count),
@@ -603,7 +638,7 @@
     )
     values = exchanged(sent, count)
     (x,) = call(
-        functools.partial(finish_kernel, count, VALUES),
+        functools.partial(finish_without, count, VALUES),
         (values, shares, members, lower, upper, maps, scaled, starts),
         (field,),
         (state, entries),

time: 88.6 us -> 85.9 us (0.970)
  waiting for transfers between devices: 4.97 us -> 2.78 us
  starting transfers between devices: 21.9 us -> 20.7 us
    ppermute x8, waiting for transfers between devices: 4.97 us -> 2.78 us  [the longest x4 1.65 us: both(): lax.ppermute(up, axis, ring(size, 1))]
    ppermute x8, starting transfers between devices: 16 us -> 14.8 us  [the longest x4 8.5 us: both(): lax.ppermute(down, axis, ring(size, -1))]
  transfers between devices with their start and end apart: 9 -> 9, of which waited for: 3 -> 2; matrix products, arithmetic and copies ran while one was open for 0% -> 0% of each run, Pallas kernels for 6% -> 7%
where the time goes in v3:
time: 85.9 us; the launch traced here: 85.5 us
  blocking collectives  49.7 us (58%)
  starting transfers between devices  20.7 us (24%)
  Pallas kernels  12.2 us (14%)
  waiting for transfers between devices  2.78 us (3%)
    all_to_all x2, blocking collectives, exchanged(): lax.all_to_all(rows, 'normal', 0, 0, axis_index_groups=groups)  49.7 us
    pallas_call x7, Pallas kernels, call(): pl.pallas_call(kernel, out_shape=[floats(a) if isinstance(a, int) else a...  12.2 us
    ppermute x4, starting transfers between devices, both(): lax.ppermute(down, axis, ring(size, -1))  8.5 us
    ppermute x4, starting transfers between devices, both(): lax.ppermute(up, axis, ring(size, 1))  6.32 us
    all_to_all x1, starting transfers between devices, exchanged(): lax.all_to_all(rows, 'normal', 0, 0, axis_index_groups=groups)  5.91 us
  transfers between devices with their start and end apart: 9, of which 2 were waited for; matrix products, arithmetic and copies ran while one was open for 0% of the time, Pallas kernels for 7%

profile of v3, /device:TPU:24, one launch (start us, length us, event | category | flops | bytes accessed | tf_op | source)
XLA Modules:
  0.0 85.5 jit_solution(18005752152114786433)
XLA Ops:
  0.0 3.0 %summary.1 = f32[304,128]{1,0:T(8,128)} custom-call(f32[1200,128]{1,0:T(8,128)} %bitcast.25, f32[1200,128]{1,0:T(8,128)} %bitcast.27), custom_call_target="tpu_custom_call" | custom-call | bytes 6000000 | tf_op jit(solution)/shard_map/summary/pallas_call | solution.py:533
  3.0 5.9 %all-to-all-start = ((f32[4,76,1,128]{3,2,1,0:T(1,128)}), f32[4,76,1,128]{3,2,1,0:T(1,128)S(1)}, u32[]{:S(2)}, u32[]{:S(2)}) async-start(f32[4,76,1,128]{3,2,1,0:T(1,128)} %bitcast.2), calls=%async_computation | async-start | bytes 311296 | tf_op jit(solution)/shard_map/all_to_all | solution.py:566
  8.9 2.6 %collective-permute-start.3 = (f32[240,128]{1,0:T(8,128)}, f32[240,128]{1,0:T(8,128)S(1)}, u32[]{:S(2)}, u32[]{:S(2)}) collective-permute-start(f32[240,128]{1,0:T(8,128)} %bitcast.31), channel_id=1, source_target_pairs={{0,3},{1,0},{2,1},{3,2},{4,7},{5,4},{6,5},{7,6},{8,11},{9,8},{10,9... | collective-permute-start | bytes 368648 | tf_op jit(solution)/shard_map/ppermute | solution.py:562
  11.5 4.4 %collective-permute-start.2 = (f32[240,128]{1,0:T(8,128)}, f32[240,128]{1,0:T(8,128)S(1)}, u32[]{:S(2)}, u32[]{:S(2)}) collective-permute-start(f32[240,128]{1,0:T(8,128)} %bitcast.32), channel_id=1, source_target_pairs={{0,1},{1,2},{2,3},{3,0},{4,5},{5,6},{6,7},{7,4},{8,9},{9,10},{10,1... | collective-permute-start | bytes 368648 | tf_op jit(solution)/shard_map/ppermute | solution.py:562
  15.9 1.4 %collective-permute-start.1 = (f32[240,128]{1,0:T(8,128)}, f32[240,128]{1,0:T(8,128)S(1)}, u32[]{:S(2)}, u32[]{:S(2)}) collective-permute-start(f32[240,128]{1,0:T(8,128)} %bitcast.33), channel_id=1, source_target_pairs={{0,28},{4,0},{8,4},{12,8},{16,12},{20,16},{24,20},{28,24},{1,29},{... | collective-permute-start | bytes 368648 | tf_op jit(solution)/shard_map/ppermute | solution.py:562
  17.3 0.0 collective-permute-start
  17.3 0.0 all-to-all-done
  17.3 4.0 %start.1 = (f32[1200,128]{1,0:T(8,128)S(1)}, f32[1200,128]{1,0:T(8,128)S(1)}, f32[240,128]{1,0:T(8,128)S(1)}, s32[48,128]{1,0:T(8,128)S(1)}, f32[240,128]{1,0:T(...) custom-call(f32[304,128]{1,0:T(8,128)S(1)} %bitcast.18, ...), custom_call_target="tpu_custom_call" | custom-call | bytes 12000000 | tf_op jit(solution)/shard_map/start/pallas_call | solution.py:533
  21.4 0.0 collective-permute-done.3.right_ref
  21.4 0.0 collective-permute-done.2.left_ref
  21.4 0.0 collective-permute-done.1.above_ref
  21.4 1.6 %collective-permute-done.below_ref = f32[240,128]{1,0:T(8,128)S(1)} collective-permute-done((f32[240,128]{1,0:T(8,128)}, f32[240,128]{1,0:T(8,128)S(1)}, u32[]{:S(2)}, u32[]{:S(2)}) %collective-permute-start) | collective-permute-done | bytes 122912 | tf_op jit(solution)/shard_map/ppermute | solution.py:562
  23.0 0.8 solve.2
  23.8 29.8 %all_to_all.15 = f32[16,29,1,128]{3,2,1,0:T(1,128)S(1)} all-to-all(f32[16,29,1,128]{3,2,1,0:T(1,128)S(1)} %bitcast.22), channel_id=1, replica_groups=mesh['normal'=16,'span'=8,'stream'=4] {'normal'}, dimensions={0} | all-to-all | bytes 475136 | tf_op jit(solution)/shard_map/all_to_all | solution.py:566
  53.7 0.8 finish.2
  54.5 0.6 collective-permute-start.5
  55.1 0.0 collective-permute-start.4
  55.1 1.9 %collective-permute-start.6 = (f32[8,128]{1,0:T(8,128)S(1)}, f32[8,128]{1,0:T(8,128)S(1)}, u32[]{:S(2)}, u32[]{:S(2)}) collective-permute-start(f32[8,128]{1,0:T(8,128)S(1)} %get-tuple-element.41), channel_id=1, source_target_pairs={{0,1},{1,2},{2,3},{3,0},{4,5},{5,6},{6,7},{7,4},{8,9},{9,10},{10,1... | collective-permute-start | bytes 12296 | tf_op jit(solution)/shard_map/ppermute | solution.py:562
  57.0 3.9 %collective-permute-start.7 = (f32[8,128]{1,0:T(8,128)S(1)}, f32[8,128]{1,0:T(8,128)S(1)}, u32[]{:S(2)}, u32[]{:S(2)}) collective-permute-start(f32[8,128]{1,0:T(8,128)S(1)} %get-tuple-element.42), channel_id=1, source_target_pairs={{0,3},{1,0},{2,1},{3,2},{4,7},{5,4},{6,5},{7,6},{8,11},{9,8},{10,9... | collective-permute-start | bytes 12296 | tf_op jit(solution)/shard_map/ppermute | solution.py:562
  60.9 1.6 %donate.1.refs_11_ = f32[240,128]{1,0:T(8,128)S(1)} custom-call(f32[240,128]{1,0:T(8,128)S(1)} %get-tuple-element.40.x_ref.refs_0_, s32[48,128]{1,0:T(8,128)S(1)} %get-tuple-element.43.donor_ref), custom_call_target="tpu_custom_call" | custom-call | bytes 6000000 | tf_op jit(solution)/shard_map/donate/pallas_call | solution.py:533
  62.6 0.0 collective-permute-done.6.refs_3_
  62.6 1.1 %collective-permute-done.7.refs_4_ = f32[8,128]{1,0:T(8,128)S(1)} collective-permute-done((f32[8,128]{1,0:T(8,128)S(1)}, f32[8,128]{1,0:T(8,128)S(1)}, u32[]{:S(2)}, u32[]{:S(2)}) %collective-permute-start.7) | collective-permute-done | bytes 4128 | tf_op jit(solution)/shard_map/ppermute | solution.py:562
  63.7 0.0 collective-permute-done.5.refs_2_
  63.7 0.0 collective-permute-done.4.refs_1_
  63.7 0.9 %solve.3 = (f32[160,128]{1,0:T(8,128)S(1)}, f32[240,128]{1,0:T(8,128)S(1)}, f32[80,128]{1,0:T(8,128)S(1)}) custom-call(f32[240,128]{1,0:T(8,128)S(1)} %get-tuple-element.40.x_ref.refs_0_, f32[240,128]{1,0:T(8,128)S(1)} %collective-permute-done.4.refs_1_, f32[240,128]{1,0:T(8,128)S(1)} %collective-permute-done.5.refs_2_, ...), custom_call_target="tpu_custom_call" | custom-call | bytes 6000000 | tf_op jit(solution)/shard_map/solve/pallas_call | solution.py:533
  64.6 19.9 %all_to_all.16 = f32[16,10,1,128]{3,2,1,0:T(1,128)S(1)} all-to-all(f32[16,10,1,128]{3,2,1,0:T(1,128)S(1)} %bitcast.23), channel_id=1, replica_groups=mesh['normal'=16,'span'=8,'stream'=4] {'normal'}, dimensions={0} | all-to-all | bytes 163840 | tf_op jit(solution)/shard_map/all_to_all | solution.py:566
  84.5 1.1 %finish.3 = f32[240,128]{1,0:T(8,128)} custom-call(f32[160,128]{1,0:T(8,128)S(1)} %bitcast.21, f32[464,128]{1,0:T(8,128)S(1)} %bitcast.17, f32[304,128]{1,0:T(8,128)S(1)} %bitcast.20, f32[1200,128]{1,0:T(8,128)S(1)} %get-tuple-element.29.lower_ref.refs_7_.refs_3_, f32[1200,128]{1,0:T(8,128)S(1)} %get-tuple-element.30.upper_ref.refs_8_.refs_4_, ...), custom_call_target="tpu_custom_call" | custom-call | bytes 3000000 | tf_op jit(solution)/shard_map/finish/pallas_call | solution.py:533
Async XLA Ops:
  3.0 14.3 %all-to-all-start = ((f32[4,76,1,128]{3,2,1,0:T(1,128)}), f32[4,76,1,128]{3,2,1,0:T(1,128)S(1)}, u32[]{:S(2)}, u32[]{:S(2)}) async-start(f32[4,76,1,128]{3,2,1,0:T(1,128)} %bitcast.2), calls=%async_computation | async-start | bytes 311296 | tf_op jit(solution)/shard_map/all_to_all | solution.py:566
  8.9 12.5 %collective-permute-start.3 = (f32[240,128]{1,0:T(8,128)}, f32[240,128]{1,0:T(8,128)S(1)}, u32[]{:S(2)}, u32[]{:S(2)}) collective-permute-start(f32[240,128]{1,0:T(8,128)} %bitcast.31), channel_id=1, source_target_pairs={{0,3},{1,0},{2,1},{3,2},{4,7},{5,4},{6,5},{7,6},{8,11},{9,8},{10,9... | collective-permute-start | bytes 368648 | tf_op jit(solution)/shard_map/ppermute | solution.py:562
  11.5 9.9 %collective-permute-start.2 = (f32[240,128]{1,0:T(8,128)}, f32[240,128]{1,0:T(8,128)S(1)}, u32[]{:S(2)}, u32[]{:S(2)}) collective-permute-start(f32[240,128]{1,0:T(8,128)} %bitcast.32), channel_id=1, source_target_pairs={{0,1},{1,2},{2,3},{3,0},{4,5},{5,6},{6,7},{7,4},{8,9},{9,10},{10,1... | collective-permute-start | bytes 368648 | tf_op jit(solution)/shard_map/ppermute | solution.py:562
  15.9 5.4 %collective-permute-start.1 = (f32[240,128]{1,0:T(8,128)}, f32[240,128]{1,0:T(8,128)S(1)}, u32[]{:S(2)}, u32[]{:S(2)}) collective-permute-start(f32[240,128]{1,0:T(8,128)} %bitcast.33), channel_id=1, source_target_pairs={{0,28},{4,0},{8,4},{12,8},{16,12},{20,16},{24,20},{28,24},{1,29},{... | collective-permute-start | bytes 368648 | tf_op jit(solution)/shard_map/ppermute | solution.py:562
  17.3 5.7 %collective-permute-start = (f32[240,128]{1,0:T(8,128)}, f32[240,128]{1,0:T(8,128)S(1)}, u32[]{:S(2)}, u32[]{:S(2)}) collective-permute-start(f32[240,128]{1,0:T(8,128)} %bitcast.34), channel_id=1, source_target_pairs={{0,4},{4,8},{8,12},{12,16},{16,20},{20,24},{24,28},{28,0},{1,5},{5... | collective-permute-start | bytes 368648 | tf_op jit(solution)/shard_map/ppermute | solution.py:562
  54.5 9.2 %collective-permute-start.5 = (f32[240,128]{1,0:T(8,128)S(1)}, f32[240,128]{1,0:T(8,128)S(1)}, u32[]{:S(2)}, u32[]{:S(2)}) collective-permute-start(f32[240,128]{1,0:T(8,128)S(1)} %get-tuple-element.40.x_ref.refs_0_), channel_id=1, source_target_pairs={{0,28},{4,0},{8,4},{12,8},{16,12},{20,16},{24,20},{28,24},{1,29},{... | collective-permute-start | bytes 368648 | tf_op jit(solution)/shard_map/ppermute | solution.py:562
  55.1 8.6 %collective-permute-start.4 = (f32[240,128]{1,0:T(8,128)S(1)}, f32[240,128]{1,0:T(8,128)S(1)}, u32[]{:S(2)}, u32[]{:S(2)}) collective-permute-start(f32[240,128]{1,0:T(8,128)S(1)} %get-tuple-element.40.x_ref.refs_0_), channel_id=1, source_target_pairs={{0,4},{4,8},{8,12},{12,16},{16,20},{20,24},{24,28},{28,0},{1,5},{5... | collective-permute-start | bytes 368648 | tf_op jit(solution)/shard_map/ppermute | solution.py:562
  55.1 7.5 %collective-permute-start.6 = (f32[8,128]{1,0:T(8,128)S(1)}, f32[8,128]{1,0:T(8,128)S(1)}, u32[]{:S(2)}, u32[]{:S(2)}) collective-permute-start(f32[8,128]{1,0:T(8,128)S(1)} %get-tuple-element.41), channel_id=1, source_target_pairs={{0,1},{1,2},{2,3},{3,0},{4,5},{5,6},{6,7},{7,4},{8,9},{9,10},{10,1... | collective-permute-start | bytes 12296 | tf_op jit(solution)/shard_map/ppermute | solution.py:562
  57.0 6.7 %collective-permute-start.7 = (f32[8,128]{1,0:T(8,128)S(1)}, f32[8,128]{1,0:T(8,128)S(1)}, u32[]{:S(2)}, u32[]{:S(2)}) collective-permute-start(f32[8,128]{1,0:T(8,128)S(1)} %get-tuple-element.42), channel_id=1, source_target_pairs={{0,3},{1,0},{2,1},{3,2},{4,7},{5,4},{6,5},{7,6},{8,11},{9,8},{10,9... | collective-permute-start | bytes 12296 | tf_op jit(solution)/shard_map/ppermute | solution.py:562

commit v4 on v2

--- a/solution.py
+++ b/solution.py
@@ -114,19 +114,36 @@
     donate(x_ref, donor_ref, donated_ref)
 
 
-def summary_kernel(lower_in, upper_in, whole_out, lower_ref, upper_ref, maps_ref, whole_ref, local_ref, moves):
-    copies = [
-        pltpu.make_async_copy(a, b, moves.at[k])
-        for k, (a, b) in enumerate(((lower_in, lower_ref), (upper_in, upper_ref)))
+def edges_of(ref):
+    lane = lax.broadcasted_iota(jnp.int32, (PIECES, LANES), 1)
+    first = last = jnp.zeros((PIECES, LANES), jnp.float32)
+    for step in range(STEPS):
+        for c, value in enumerate(vector_at(ref, step)):
+            here = lane == step * COMP + c
+            first = jnp.where(here, jnp.broadcast_to(value[:, :1], (PIECES, LANES)), first)
+            last = jnp.where(here, jnp.broadcast_to(value[:, -1:], (PIECES, LANES)), last)
+    return first, last
+
+
+def summary_kernel(*refs):
+    given, results, kept, (maps_ref, local_ref, moves) = refs[:3], refs[3:6], refs[6:12], refs[12:]
+    coming = [pltpu.make_async_copy(a, b, moves.at[k]) for k, (a, b) in enumerate(zip(given, kept))]
+    leaving = [
+        pltpu.make_async_copy(a, b, moves.at[3 + k]) for k, (a, b) in enumerate(zip(kept[3:], results))
     ]
-    for copy in copies:
+    x_ref, lower_ref, upper_ref, first_ref, last_ref, whole_ref = kept
+    for copy in coming:
         copy.start()
-    for copy in copies:
+    coming[0].wait()
+    first_ref[...], last_ref[...] = edges_of(x_ref)
+    for copy in leaving[:2]:
+        copy.start()
+    for copy in coming[1:]:
         copy.wait()
     make_maps(lower_ref, upper_ref, maps_ref, whole_ref, local_ref)
-    copy = pltpu.make_async_copy(whole_ref, whole_out, moves.at[2])
-    copy.start()
-    copy.wait()
+    leaving[2].start()
+    for copy in leaving:
+        copy.wait()
 
 
 def start_kernel(*refs):
@@ -138,14 +155,14 @@
     ]
     for copy in copies:
         copy.start()
-    lower_ref, upper_ref, x_ref, donor_ref = kept[:4]
+    x_ref, donor_ref, lower_ref, upper_ref = kept[:4]
+    group_maps(members_ref, share_ref, outer_ref, group_ref, work_ref)
     for copy in copies[:2]:
         copy.wait()
-    make_maps(lower_ref, upper_ref, maps_ref, whole_ref, local_ref)
-    group_maps(members_ref, share_ref, outer_ref, group_ref, work_ref)
+    donate(x_ref, donor_ref, donated_ref)
     for copy in copies[2:4]:
         copy.wait()
-    donate(x_ref, donor_ref, donated_ref)
+    make_maps(lower_ref, upper_ref, maps_ref, whole_ref, local_ref)
     for copy in copies[4:]:
         copy.wait()
 
@@ -256,14 +273,15 @@
 
     def forward(step, state):
         x = vector_at(x_ref, step)
-        before = [
-            pltpu.roll(jnp.where(lane == LANES - 1, a, b), 1, 1)
-            for a, b in zip(vector_at(left_ref, step), x)
-        ]
-        after = [
-            pltpu.roll(jnp.where(lane == 0, a, b), LANES - 1, 1)
-            for a, b in zip(vector_at(right_ref, step), x)
-        ]
+        before, after = [], []
+        for c in SIZES:
+            place = jnp.full((PIECES, LANES), step * COMP + c, jnp.int32)
+            for out, edges_ref, turn, at in (
+                (before, left_ref, 1, 0),
+                (after, right_ref, LANES - 1, LANES - 1),
+            ):
+                edge = jnp.take_along_axis(edges_ref[...], place, axis=1, mode="promise_in_bounds")
+                out.append(jnp.where(lane == at, edge, pltpu.roll(x[c], turn, 1)))
         near = [vector_at(below_ref, step), vector_at(above_ref, step), before, after]
         rhs = vector_at(source_ref, step)
         for direc in range(4):
@@ -392,6 +410,8 @@
     scaled_ref,
     starts_ref,
     out_ref,
+    first_ref,
+    last_ref,
     states_ref,
     entry_ref,
 ):
@@ -474,6 +494,12 @@
         return tuple(state)
 
     lax.fori_loop(0, STEPS, behind, tuple(x_start))
+    if first_ref is not None:
+        first_ref[...], last_ref[...] = edges_of(out_ref)
+
+
+def finish_without(count, slot, *refs):
+    finish_kernel(count, slot, *refs[:9], None, None, *refs[9:])
 
 
 def floats(rows):
@@ -519,12 +545,9 @@
     field = POINTS * COMP
     state = STEPS * COMP * PIECES
 
-    def around(x):
-        return [
-            lax.ppermute(x, axis, ring(lax.axis_size(axis), step))
-            for axis in ("span", "stream")
-            for step in (1, -1)
-        ]
+    def both(up, down, axis):
+        size = lax.axis_size(axis)
+        return [lax.ppermute(up, axis, ring(size, 1)), lax.ppermute(down, axis, ring(size, -1))]
 
     def exchanged(rows, parts, groups=None):
         rows = rows.reshape(parts, -1, 1, LANES)
@@ -535,26 +558,29 @@
     whole_rows = MEMBERS * PADDED
     entries = (count // MEMBERS + MEMBERS) * PIECES
 
-    (whole,) = call(
+    first, last, whole = call(
         summary_kernel,
-        (lower, upper),
-        (whole_rows,),
+        (x, lower, upper),
+        (PIECES, PIECES, whole_rows),
         (
+            x.shape[0],
             lower.shape[0],
             upper.shape[0],
+            PIECES,
+            PIECES,
+            whole_rows,
             maps_rows,
-            whole_rows,
             local_rows,
-            pltpu.SemaphoreType.DMA((3,)),
+            pltpu.SemaphoreType.DMA((6,)),
         ),
         "summary",
         2,
-        far=(0, 1, 2),
+        far=range(6),
     )
     groups = [list(range(k, k + MEMBERS)) for k in range(0, count, MEMBERS)]
     members = exchanged(whole, MEMBERS, groups)
-    near = around(x)
-    given = (lower, upper, x, donor, source, pivot, coupling, iblank)
+    near = both(x, x, "span") + both(last, first, "stream")
+    given = (x, donor, lower, upper, source, pivot, coupling, iblank)
     *given, donated, maps, share, outer = call(
         start_kernel,
         (members, *given),
@@ -571,7 +597,7 @@
         4,
         far=range(1, len(given) + 1),
     )
-    lower, upper, x, donor, source, pivot, coupling, iblank = given
+    x, donor, lower, upper, source, pivot, coupling, iblank = given
     fixed = (source, pivot, lower, upper, coupling, iblank)
     sent, scaled, starts = call(
         functools.partial(solve_kernel, count),
@@ -582,16 +608,16 @@
         2,
     )
     shares = exchanged(sent, count)
-    (x,) = call(
+    x, first, last = call(
         functools.partial(finish_kernel, count, SLOT),
         (shares, shares, members, lower, upper, maps, scaled, starts),
-        (field,),
+        (field, PIECES, PIECES),
         (state, entries),
         "finish",
         1,
     )
 
-    near = around(x)
+    near = both(x, x, "span") + both(last, first, "stream")
     (donated,) = call(donate_kernel, (x, donor), (state,), (), "donate", 2)
     sent, scaled, starts = call(
         functools.partial(solve_without, count),
@@ -603,7 +629,7 @@
     )
     values = exchanged(sent, count)
     (x,) = call(
-        functools.partial(finish_kernel, count, VALUES),
+        functools.partial(finish_without, count, VALUES),
         (values, shares, members, lower, upper, maps, scaled, starts),
         (field,),
         (state, entries),

time: 88.6 us -> 85.6 us (0.966)
  waiting for transfers between devices: 4.97 us -> 3.4 us
  starting transfers between devices: 21.9 us -> 20.9 us
    ppermute x8, waiting for transfers between devices: 4.97 us -> 3.4 us  [the longest x4 3.39 us: both(): lax.ppermute(down, axis, ring(size, -1))]
    ppermute x8, starting transfers between devices: 16 us -> 15 us  [the longest x4 7.96 us: both(): lax.ppermute(down, axis, ring(size, -1))]
  transfers between devices with their start and end apart: 9 -> 9, of which waited for: 3 -> 2; matrix products, arithmetic and copies ran while one was open for 0% -> 0% of each run, Pallas kernels for 6% -> 6%
where the time goes in v4:
time: 85.6 us; the launch traced here: 85.2 us
  blocking collectives  49 us (57%)
  starting transfers between devices  20.9 us (24%)
  Pallas kernels  11.8 us (14%)
  waiting for transfers between devices  3.4 us (4%)
    all_to_all x2, blocking collectives, exchanged(): lax.all_to_all(rows, 'normal', 0, 0, axis_index_groups=groups)  49 us
    pallas_call x7, Pallas kernels, call(): pl.pallas_call(kernel, out_shape=[floats(a) if isinstance(a, int) else a...  11.8 us
    ppermute x4, starting transfers between devices, both(): lax.ppermute(down, axis, ring(size, -1))  7.96 us
    ppermute x4, starting transfers between devices, both(): lax.ppermute(up, axis, ring(size, 1))  7.01 us
    all_to_all x1, starting transfers between devices, exchanged(): lax.all_to_all(rows, 'normal', 0, 0, axis_index_groups=groups)  5.91 us
    ppermute x4, waiting for transfers between devices, both(): lax.ppermute(down, axis, ring(size, -1))  3.39 us
  transfers between devices with their start and end apart: 9, of which 2 were waited for; matrix products, arithmetic and copies ran while one was open for 0% of the time, Pallas kernels for 6%

profile of v4, /device:TPU:24, one launch (start us, length us, event | category | flops | bytes accessed | tf_op | source)
XLA Modules:
  0.0 85.2 jit_solution(9981472976332545881)
XLA Ops:
  0.0 3.1 %summary.1 = (f32[8,128]{1,0:T(8,128)S(1)}, f32[8,128]{1,0:T(8,128)S(1)}, f32[304,128]{1,0:T(8,128)}) custom-call(f32[240,128]{1,0:T(8,128)} %bitcast.30, f32[1200,128]{1,0:T(8,128)} %bitcast.25, f32[1200,128]{1,0:T(8,128)} %bitcast.27), custom_call_target="tpu_custom_call" | custom-call | bytes 6000000 | tf_op jit(solution)/shard_map/summary/pallas_call | solution.py:521
  3.1 5.9 %all-to-all-start = ((f32[4,76,1,128]{3,2,1,0:T(1,128)}), f32[4,76,1,128]{3,2,1,0:T(1,128)S(1)}, u32[]{:S(2)}, u32[]{:S(2)}) async-start(f32[4,76,1,128]{3,2,1,0:T(1,128)} %bitcast.3), calls=%async_computation | async-start | bytes 311296 | tf_op jit(solution)/shard_map/all_to_all | solution.py:554
  9.0 1.9 %collective-permute-start.1 = (f32[240,128]{1,0:T(8,128)}, f32[240,128]{1,0:T(8,128)S(1)}, u32[]{:S(2)}, u32[]{:S(2)}) collective-permute-start(f32[240,128]{1,0:T(8,128)} %bitcast.31), channel_id=1, source_target_pairs={{0,28},{4,0},{8,4},{12,8},{16,12},{20,16},{24,20},{28,24},{1,29},{... | collective-permute-start | bytes 368648 | tf_op jit(solution)/shard_map/ppermute | solution.py:550
  10.9 0.0 collective-permute-start
  10.9 3.5 %collective-permute-start.2 = (f32[8,128]{1,0:T(8,128)S(1)}, f32[8,128]{1,0:T(8,128)S(1)}, u32[]{:S(2)}, u32[]{:S(2)}) collective-permute-start(f32[8,128]{1,0:T(8,128)S(1)} %get-tuple-element.31), channel_id=1, source_target_pairs={{0,1},{1,2},{2,3},{3,0},{4,5},{5,6},{6,7},{7,4},{8,9},{9,10},{10,1... | collective-permute-start | bytes 12296 | tf_op jit(solution)/shard_map/ppermute | solution.py:550
  14.4 2.3 %collective-permute-start.3 = (f32[8,128]{1,0:T(8,128)S(1)}, f32[8,128]{1,0:T(8,128)S(1)}, u32[]{:S(2)}, u32[]{:S(2)}) collective-permute-start(f32[8,128]{1,0:T(8,128)S(1)} %get-tuple-element.32), channel_id=1, source_target_pairs={{0,3},{1,0},{2,1},{3,2},{4,7},{5,4},{6,5},{7,6},{8,11},{9,8},{10,9... | collective-permute-start | bytes 12296 | tf_op jit(solution)/shard_map/ppermute | solution.py:550
  16.7 0.0 all-to-all-done
  16.8 3.7 %start.1 = (f32[240,128]{1,0:T(8,128)S(1)}, s32[48,128]{1,0:T(8,128)S(1)}, f32[1200,128]{1,0:T(8,128)S(1)}, f32[1200,128]{1,0:T(8,128)S(1)}, f32[240,128]{1,0:T(...) custom-call(f32[304,128]{1,0:T(8,128)S(1)} %bitcast.18, ...), custom_call_target="tpu_custom_call" | custom-call | bytes 12000000 | tf_op jit(solution)/shard_map/start/pallas_call | solution.py:521
  20.4 0.0 collective-permute-done.2.left_ref
  20.4 0.7 collective-permute-done.3.right_ref
  21.2 0.0 collective-permute-done.1.above_ref
  21.2 0.0 collective-permute-done.below_ref
  21.2 0.9 %solve.2 = (f32[464,128]{1,0:T(8,128)S(1)}, f32[240,128]{1,0:T(8,128)S(1)}, f32[80,128]{1,0:T(8,128)S(1)}) custom-call(f32[240,128]{1,0:T(8,128)S(1)} %get-tuple-element.30.x_ref, f32[240,128]{1,0:T(8,128)S(1)} %collective-permute-done.below_ref, f32[240,128]{1,0:T(8,128)S(1)} %collective-permute-done.1.above_ref, ...), custom_call_target="tpu_custom_call" | custom-call | bytes 6000000 | tf_op jit(solution)/shard_map/solve/pallas_call | solution.py:521
  22.1 29.4 %all_to_all.15 = f32[16,29,1,128]{3,2,1,0:T(1,128)S(1)} all-to-all(f32[16,29,1,128]{3,2,1,0:T(1,128)S(1)} %bitcast.22), channel_id=1, replica_groups=mesh['normal'=16,'span'=8,'stream'=4] {'normal'}, dimensions={0} | all-to-all | bytes 475136 | tf_op jit(solution)/shard_map/all_to_all | solution.py:554
  51.5 0.5 finish.2
  52.0 1.4 %collective-permute-start.5 = (f32[240,128]{1,0:T(8,128)S(1)}, f32[240,128]{1,0:T(8,128)S(1)}, u32[]{:S(2)}, u32[]{:S(2)}) collective-permute-start(f32[240,128]{1,0:T(8,128)S(1)} %get-tuple-element.46.x_ref.refs_0_), channel_id=1, source_target_pairs={{0,28},{4,0},{8,4},{12,8},{16,12},{20,16},{24,20},{28,24},{1,29},{... | collective-permute-start | bytes 368648 | tf_op jit(solution)/shard_map/ppermute | solution.py:550
  53.4 0.0 collective-permute-start.4
  53.4 3.5 %collective-permute-start.6 = (f32[8,128]{1,0:T(8,128)S(1)}, f32[8,128]{1,0:T(8,128)S(1)}, u32[]{:S(2)}, u32[]{:S(2)}) collective-permute-start(f32[8,128]{1,0:T(8,128)S(1)} %get-tuple-element.47), channel_id=1, source_target_pairs={{0,1},{1,2},{2,3},{3,0},{4,5},{5,6},{6,7},{7,4},{8,9},{9,10},{10,1... | collective-permute-start | bytes 12296 | tf_op jit(solution)/shard_map/ppermute | solution.py:550
  56.9 2.4 %collective-permute-start.7 = (f32[8,128]{1,0:T(8,128)S(1)}, f32[8,128]{1,0:T(8,128)S(1)}, u32[]{:S(2)}, u32[]{:S(2)}) collective-permute-start(f32[8,128]{1,0:T(8,128)S(1)} %get-tuple-element.48), channel_id=1, source_target_pairs={{0,3},{1,0},{2,1},{3,2},{4,7},{5,4},{6,5},{7,6},{8,11},{9,8},{10,9... | collective-permute-start | bytes 12296 | tf_op jit(solution)/shard_map/ppermute | solution.py:550
  59.3 1.6 %donate.1.refs_11_ = f32[240,128]{1,0:T(8,128)S(1)} custom-call(f32[240,128]{1,0:T(8,128)S(1)} %get-tuple-element.46.x_ref.refs_0_, s32[48,128]{1,0:T(8,128)S(1)} %get-tuple-element.49.donor_ref), custom_call_target="tpu_custom_call" | custom-call | bytes 6000000 | tf_op jit(solution)/shard_map/donate/pallas_call | solution.py:521
  60.9 0.0 collective-permute-done.6.refs_3_
  60.9 2.7 %collective-permute-done.7.refs_4_ = f32[8,128]{1,0:T(8,128)S(1)} collective-permute-done((f32[8,128]{1,0:T(8,128)S(1)}, f32[8,128]{1,0:T(8,128)S(1)}, u32[]{:S(2)}, u32[]{:S(2)}) %collective-permute-start.7) | collective-permute-done | bytes 4128 | tf_op jit(solution)/shard_map/ppermute | solution.py:550
  63.6 0.0 collective-permute-done.5.refs_2_
  63.6 0.0 collective-permute-done.4.refs_1_
  63.6 0.9 %solve.3 = (f32[160,128]{1,0:T(8,128)S(1)}, f32[240,128]{1,0:T(8,128)S(1)}, f32[80,128]{1,0:T(8,128)S(1)}) custom-call(f32[240,128]{1,0:T(8,128)S(1)} %get-tuple-element.46.x_ref.refs_0_, f32[240,128]{1,0:T(8,128)S(1)} %collective-permute-done.4.refs_1_, f32[240,128]{1,0:T(8,128)S(1)} %collective-permute-done.5.refs_2_, ...), custom_call_target="tpu_custom_call" | custom-call | bytes 6000000 | tf_op jit(solution)/shard_map/solve/pallas_call | solution.py:521
  64.5 19.6 %all_to_all.16 = f32[16,10,1,128]{3,2,1,0:T(1,128)S(1)} all-to-all(f32[16,10,1,128]{3,2,1,0:T(1,128)S(1)} %bitcast.23), channel_id=1, replica_groups=mesh['normal'=16,'span'=8,'stream'=4] {'normal'}, dimensions={0} | all-to-all | bytes 163840 | tf_op jit(solution)/shard_map/all_to_all | solution.py:554
  84.1 1.1 %finish.3 = f32[240,128]{1,0:T(8,128)} custom-call(f32[160,128]{1,0:T(8,128)S(1)} %bitcast.21, f32[464,128]{1,0:T(8,128)S(1)} %bitcast.17, f32[304,128]{1,0:T(8,128)S(1)} %bitcast.20, f32[1200,128]{1,0:T(8,128)S(1)} %get-tuple-element.35.lower_ref.refs_7_.refs_3_, f32[1200,128]{1,0:T(8,128)S(1)} %get-tuple-element.36.upper_ref.refs_8_.refs_4_, ...), custom_call_target="tpu_custom_call" | custom-call | bytes 3000000 | tf_op jit(solution)/shard_map/finish/pallas_call | solution.py:521
Async XLA Ops:
  3.1 13.7 %all-to-all-start = ((f32[4,76,1,128]{3,2,1,0:T(1,128)}), f32[4,76,1,128]{3,2,1,0:T(1,128)S(1)}, u32[]{:S(2)}, u32[]{:S(2)}) async-start(f32[4,76,1,128]{3,2,1,0:T(1,128)} %bitcast.3), calls=%async_computation | async-start | bytes 311296 | tf_op jit(solution)/shard_map/all_to_all | solution.py:554
  9.0 12.2 %collective-permute-start.1 = (f32[240,128]{1,0:T(8,128)}, f32[240,128]{1,0:T(8,128)S(1)}, u32[]{:S(2)}, u32[]{:S(2)}) collective-permute-start(f32[240,128]{1,0:T(8,128)} %bitcast.31), channel_id=1, source_target_pairs={{0,28},{4,0},{8,4},{12,8},{16,12},{20,16},{24,20},{28,24},{1,29},{... | collective-permute-start | bytes 368648 | tf_op jit(solution)/shard_map/ppermute | solution.py:550
  10.9 10.3 %collective-permute-start = (f32[240,128]{1,0:T(8,128)}, f32[240,128]{1,0:T(8,128)S(1)}, u32[]{:S(2)}, u32[]{:S(2)}) collective-permute-start(f32[240,128]{1,0:T(8,128)} %bitcast.32), channel_id=1, source_target_pairs={{0,4},{4,8},{8,12},{12,16},{16,20},{20,24},{24,28},{28,0},{1,5},{5... | collective-permute-start | bytes 368648 | tf_op jit(solution)/shard_map/ppermute | solution.py:550
  10.9 9.5 %collective-permute-start.2 = (f32[8,128]{1,0:T(8,128)S(1)}, f32[8,128]{1,0:T(8,128)S(1)}, u32[]{:S(2)}, u32[]{:S(2)}) collective-permute-start(f32[8,128]{1,0:T(8,128)S(1)} %get-tuple-element.31), channel_id=1, source_target_pairs={{0,1},{1,2},{2,3},{3,0},{4,5},{5,6},{6,7},{7,4},{8,9},{9,10},{10,1... | collective-permute-start | bytes 12296 | tf_op jit(solution)/shard_map/ppermute | solution.py:550
  14.4 6.7 %collective-permute-start.3 = (f32[8,128]{1,0:T(8,128)S(1)}, f32[8,128]{1,0:T(8,128)S(1)}, u32[]{:S(2)}, u32[]{:S(2)}) collective-permute-start(f32[8,128]{1,0:T(8,128)S(1)} %get-tuple-element.32), channel_id=1, source_target_pairs={{0,3},{1,0},{2,1},{3,2},{4,7},{5,4},{6,5},{7,6},{8,11},{9,8},{10,9... | collective-permute-start | bytes 12296 | tf_op jit(solution)/shard_map/ppermute | solution.py:550
  52.0 11.6 %collective-permute-start.5 = (f32[240,128]{1,0:T(8,128)S(1)}, f32[240,128]{1,0:T(8,128)S(1)}, u32[]{:S(2)}, u32[]{:S(2)}) collective-permute-start(f32[240,128]{1,0:T(8,128)S(1)} %get-tuple-element.46.x_ref.refs_0_), channel_id=1, source_target_pairs={{0,28},{4,0},{8,4},{12,8},{16,12},{20,16},{24,20},{28,24},{1,29},{... | collective-permute-start | bytes 368648 | tf_op jit(solution)/shard_map/ppermute | solution.py:550
  53.4 10.2 %collective-permute-start.4 = (f32[240,128]{1,0:T(8,128)S(1)}, f32[240,128]{1,0:T(8,128)S(1)}, u32[]{:S(2)}, u32[]{:S(2)}) collective-permute-start(f32[240,128]{1,0:T(8,128)S(1)} %get-tuple-element.46.x_ref.refs_0_), channel_id=1, source_target_pairs={{0,4},{4,8},{8,12},{12,16},{16,20},{20,24},{24,28},{28,0},{1,5},{5... | collective-permute-start | bytes 368648 | tf_op jit(solution)/shard_map/ppermute | solution.py:550
  53.4 7.5 %collective-permute-start.6 = (f32[8,128]{1,0:T(8,128)S(1)}, f32[8,128]{1,0:T(8,128)S(1)}, u32[]{:S(2)}, u32[]{:S(2)}) collective-permute-start(f32[8,128]{1,0:T(8,128)S(1)} %get-tuple-element.47), channel_id=1, source_target_pairs={{0,1},{1,2},{2,3},{3,0},{4,5},{5,6},{6,7},{7,4},{8,9},{9,10},{10,1... | collective-permute-start | bytes 12296 | tf_op jit(solution)/shard_map/ppermute | solution.py:550
  56.9 6.7 %collective-permute-start.7 = (f32[8,128]{1,0:T(8,128)S(1)}, f32[8,128]{1,0:T(8,128)S(1)}, u32[]{:S(2)}, u32[]{:S(2)}) collective-permute-start(f32[8,128]{1,0:T(8,128)S(1)} %get-tuple-element.48), channel_id=1, source_target_pairs={{0,3},{1,0},{2,1},{3,2},{4,7},{5,4},{6,5},{7,6},{8,11},{9,8},{10,9... | collective-permute-start | bytes 12296 | tf_op jit(solution)/shard_map/ppermute | solution.py:550

commit v5 on v4

--- a/solution.py
+++ b/solution.py
@@ -193,7 +193,7 @@
         put_map(local_ref, step, state)
         return pack(state)
 
-    ahead = unpack(lax.fori_loop(1, STEPS, forward, pack(first)))
+    ahead = unpack(lax.fori_loop(1, STEPS, forward, pack(first), unroll=True))
 
     def backward(count, carry):
         behind, fold = unpack(carry[:BLOCK]), unpack(carry[BLOCK:])
@@ -205,7 +205,7 @@
 
     last = block_at(upper_ref, STEPS - 1)
     start = pack(each(lambda a: -a, last)) + pack(map_at(local_ref, STEPS - 1))
-    carry = lax.fori_loop(1, STEPS, backward, start)
+    carry = lax.fori_loop(1, STEPS, backward, start, unroll=True)
     behind, fold = unpack(carry[:BLOCK]), unpack(carry[BLOCK:])
     put_map(maps_ref, FOLD, fold)
 
@@ -300,14 +300,14 @@
         put_packed(states_ref, step, state)
         return tuple(state)
 
-    ahead = list(lax.fori_loop(0, STEPS, forward, (zero,) * COMP))
+    ahead = list(lax.fori_loop(0, STEPS, forward, (zero,) * COMP, unroll=True))
 
     def backward(count, state):
         step = STEPS - 1 - count
         y = packed_at(states_ref, step)
         return tuple(less(y, times(block_at(upper_ref, step), state)))
 
-    behind = list(lax.fori_loop(0, STEPS, backward, (zero,) * COMP))
+    behind = list(lax.fori_loop(0, STEPS, backward, (zero,) * COMP, unroll=True))
 
     for level, shift in enumerate((1, 2, 4)):
         ahead = add(ahead, times(map_at(maps_ref, FWD0 + level), [moved(a, shift) for a in ahead]))
@@ -484,7 +484,7 @@
         put_packed(states_ref, step, state)
         return tuple(state)
 
-    lax.fori_loop(0, STEPS, ahead, tuple(y_start))
+    lax.fori_loop(0, STEPS, ahead, tuple(y_start), unroll=True)
 
     def behind(turn, state):
         step = STEPS - 1 - turn
@@ -493,7 +493,7 @@
             out_ref[pl.ds(step * COMP + c, PIECES, stride=STEPS * COMP), :] = state[c]
         return tuple(state)
 
-    lax.fori_loop(0, STEPS, behind, tuple(x_start))
+    lax.fori_loop(0, STEPS, behind, tuple(x_start), unroll=True)
     if first_ref is not None:
         first_ref[...], last_ref[...] = edges_of(out_ref)
 

time: 85.6 us -> 84.3 us (0.985)
  Pallas kernels: 11.8 us -> 10.5 us
    pallas_call x7, Pallas kernels: 11.8 us -> 10.5 us  [call(): pl.pallas_call(kernel, out_shape=[floats(a) if isinstance(a, int) else a...]
where the time goes in v5:
time: 84.3 us; the launch traced here: 83.9 us
  blocking collectives  48.9 us (58%)
  starting transfers between devices  20.9 us (25%)
  Pallas kernels  10.5 us (12%)
  waiting for transfers between devices  3.49 us (4%)
    all_to_all x2, blocking collectives, exchanged(): lax.all_to_all(rows, 'normal', 0, 0, axis_index_groups=groups)  48.9 us
    pallas_call x7, Pallas kernels, call(): pl.pallas_call(kernel, out_shape=[floats(a) if isinstance(a, int) else a...  10.5 us
    ppermute x4, starting transfers between devices, both(): lax.ppermute(down, axis, ring(size, -1))  7.96 us
    ppermute x4, starting transfers between devices, both(): lax.ppermute(up, axis, ring(size, 1))  7.01 us
    all_to_all x1, starting transfers between devices, exchanged(): lax.all_to_all(rows, 'normal', 0, 0, axis_index_groups=groups)  5.91 us
    ppermute x4, waiting for transfers between devices, both(): lax.ppermute(down, axis, ring(size, -1))  3.48 us
  transfers between devices with their start and end apart: 9, of which 2 were waited for; matrix products, arithmetic and copies ran while one was open for 0% of the time, Pallas kernels for 6%

profile of v5, /device:TPU:24, one launch (start us, length us, event | category | flops | bytes accessed | tf_op | source)
XLA Modules:
  0.0 83.9 jit_solution(5336703727853972865)
XLA Ops:
  0.0 3.0 %summary.1 = (f32[8,128]{1,0:T(8,128)S(1)}, f32[8,128]{1,0:T(8,128)S(1)}, f32[304,128]{1,0:T(8,128)}) custom-call(f32[240,128]{1,0:T(8,128)} %bitcast.30, f32[1200,128]{1,0:T(8,128)} %bitcast.25, f32[1200,128]{1,0:T(8,128)} %bitcast.27), custom_call_target="tpu_custom_call" | custom-call | bytes 6000000 | tf_op jit(solution)/shard_map/summary/pallas_call | solution.py:521
  3.0 5.9 %all-to-all-start = ((f32[4,76,1,128]{3,2,1,0:T(1,128)}), f32[4,76,1,128]{3,2,1,0:T(1,128)S(1)}, u32[]{:S(2)}, u32[]{:S(2)}) async-start(f32[4,76,1,128]{3,2,1,0:T(1,128)} %bitcast.3), calls=%async_computation | async-start | bytes 311296 | tf_op jit(solution)/shard_map/all_to_all | solution.py:554
  8.9 1.9 %collective-permute-start.1 = (f32[240,128]{1,0:T(8,128)}, f32[240,128]{1,0:T(8,128)S(1)}, u32[]{:S(2)}, u32[]{:S(2)}) collective-permute-start(f32[240,128]{1,0:T(8,128)} %bitcast.31), channel_id=1, source_target_pairs={{0,28},{4,0},{8,4},{12,8},{16,12},{20,16},{24,20},{28,24},{1,29},{... | collective-permute-start | bytes 368648 | tf_op jit(solution)/shard_map/ppermute | solution.py:550
  10.8 0.0 collective-permute-start
  10.8 3.5 %collective-permute-start.2 = (f32[8,128]{1,0:T(8,128)S(1)}, f32[8,128]{1,0:T(8,128)S(1)}, u32[]{:S(2)}, u32[]{:S(2)}) collective-permute-start(f32[8,128]{1,0:T(8,128)S(1)} %get-tuple-element.31), channel_id=1, source_target_pairs={{0,1},{1,2},{2,3},{3,0},{4,5},{5,6},{6,7},{7,4},{8,9},{9,10},{10,1... | collective-permute-start | bytes 12296 | tf_op jit(solution)/shard_map/ppermute | solution.py:550
  14.4 2.3 %collective-permute-start.3 = (f32[8,128]{1,0:T(8,128)S(1)}, f32[8,128]{1,0:T(8,128)S(1)}, u32[]{:S(2)}, u32[]{:S(2)}) collective-permute-start(f32[8,128]{1,0:T(8,128)S(1)} %get-tuple-element.32), channel_id=1, source_target_pairs={{0,3},{1,0},{2,1},{3,2},{4,7},{5,4},{6,5},{7,6},{8,11},{9,8},{10,9... | collective-permute-start | bytes 12296 | tf_op jit(solution)/shard_map/ppermute | solution.py:550
  16.7 0.0 all-to-all-done
  16.7 3.6 %start.1 = (f32[240,128]{1,0:T(8,128)S(1)}, s32[48,128]{1,0:T(8,128)S(1)}, f32[1200,128]{1,0:T(8,128)S(1)}, f32[1200,128]{1,0:T(8,128)S(1)}, f32[240,128]{1,0:T(...) custom-call(f32[304,128]{1,0:T(8,128)S(1)} %bitcast.18, ...), custom_call_target="tpu_custom_call" | custom-call | bytes 12000000 | tf_op jit(solution)/shard_map/start/pallas_call | solution.py:521
  20.3 0.0 collective-permute-done.2.left_ref
  20.3 0.8 collective-permute-done.3.right_ref
  21.1 0.0 collective-permute-done.1.above_ref
  21.1 0.0 collective-permute-done.below_ref
  21.1 0.5 solve.2
  21.5 29.3 %all_to_all.15 = f32[16,29,1,128]{3,2,1,0:T(1,128)S(1)} all-to-all(f32[16,29,1,128]{3,2,1,0:T(1,128)S(1)} %bitcast.22), channel_id=1, replica_groups=mesh['normal'=16,'span'=8,'stream'=4] {'normal'}, dimensions={0} | all-to-all | bytes 475136 | tf_op jit(solution)/shard_map/all_to_all | solution.py:554
  50.9 0.4 finish.2
  51.3 1.4 %collective-permute-start.5 = (f32[240,128]{1,0:T(8,128)S(1)}, f32[240,128]{1,0:T(8,128)S(1)}, u32[]{:S(2)}, u32[]{:S(2)}) collective-permute-start(f32[240,128]{1,0:T(8,128)S(1)} %get-tuple-element.46.x_ref.refs_0_), channel_id=1, source_target_pairs={{0,28},{4,0},{8,4},{12,8},{16,12},{20,16},{24,20},{28,24},{1,29},{... | collective-permute-start | bytes 368648 | tf_op jit(solution)/shard_map/ppermute | solution.py:550
  52.7 0.0 collective-permute-start.4
  52.7 3.5 %collective-permute-start.6 = (f32[8,128]{1,0:T(8,128)S(1)}, f32[8,128]{1,0:T(8,128)S(1)}, u32[]{:S(2)}, u32[]{:S(2)}) collective-permute-start(f32[8,128]{1,0:T(8,128)S(1)} %get-tuple-element.47), channel_id=1, source_target_pairs={{0,1},{1,2},{2,3},{3,0},{4,5},{5,6},{6,7},{7,4},{8,9},{9,10},{10,1... | collective-permute-start | bytes 12296 | tf_op jit(solution)/shard_map/ppermute | solution.py:550
  56.2 2.4 %collective-permute-start.7 = (f32[8,128]{1,0:T(8,128)S(1)}, f32[8,128]{1,0:T(8,128)S(1)}, u32[]{:S(2)}, u32[]{:S(2)}) collective-permute-start(f32[8,128]{1,0:T(8,128)S(1)} %get-tuple-element.48), channel_id=1, source_target_pairs={{0,3},{1,0},{2,1},{3,2},{4,7},{5,4},{6,5},{7,6},{8,11},{9,8},{10,9... | collective-permute-start | bytes 12296 | tf_op jit(solution)/shard_map/ppermute | solution.py:550
  58.5 1.6 %donate.1.refs_11_ = f32[240,128]{1,0:T(8,128)S(1)} custom-call(f32[240,128]{1,0:T(8,128)S(1)} %get-tuple-element.46.x_ref.refs_0_, s32[48,128]{1,0:T(8,128)S(1)} %get-tuple-element.49.donor_ref), custom_call_target="tpu_custom_call" | custom-call | bytes 6000000 | tf_op jit(solution)/shard_map/donate/pallas_call | solution.py:521
  60.2 0.0 collective-permute-done.6.refs_3_
  60.2 2.7 %collective-permute-done.7.refs_4_ = f32[8,128]{1,0:T(8,128)S(1)} collective-permute-done((f32[8,128]{1,0:T(8,128)S(1)}, f32[8,128]{1,0:T(8,128)S(1)}, u32[]{:S(2)}, u32[]{:S(2)}) %collective-permute-start.7) | collective-permute-done | bytes 4128 | tf_op jit(solution)/shard_map/ppermute | solution.py:550
  62.9 0.0 collective-permute-done.5.refs_2_
  62.9 0.0 collective-permute-done.4.refs_1_
  62.9 0.4 solve.3
  63.3 19.6 %all_to_all.16 = f32[16,10,1,128]{3,2,1,0:T(1,128)S(1)} all-to-all(f32[16,10,1,128]{3,2,1,0:T(1,128)S(1)} %bitcast.23), channel_id=1, replica_groups=mesh['normal'=16,'span'=8,'stream'=4] {'normal'}, dimensions={0} | all-to-all | bytes 163840 | tf_op jit(solution)/shard_map/all_to_all | solution.py:554
  82.9 1.0 %finish.3 = f32[240,128]{1,0:T(8,128)} custom-call(f32[160,128]{1,0:T(8,128)S(1)} %bitcast.21, f32[464,128]{1,0:T(8,128)S(1)} %bitcast.17, f32[304,128]{1,0:T(8,128)S(1)} %bitcast.20, f32[1200,128]{1,0:T(8,128)S(1)} %get-tuple-element.35.lower_ref.refs_7_.refs_3_, f32[1200,128]{1,0:T(8,128)S(1)} %get-tuple-element.36.upper_ref.refs_8_.refs_4_, ...), custom_call_target="tpu_custom_call" | custom-call | bytes 3000000 | tf_op jit(solution)/shard_map/finish/pallas_call | solution.py:521
Async XLA Ops:
  3.0 13.7 %all-to-all-start = ((f32[4,76,1,128]{3,2,1,0:T(1,128)}), f32[4,76,1,128]{3,2,1,0:T(1,128)S(1)}, u32[]{:S(2)}, u32[]{:S(2)}) async-start(f32[4,76,1,128]{3,2,1,0:T(1,128)} %bitcast.3), calls=%async_computation | async-start | bytes 311296 | tf_op jit(solution)/shard_map/all_to_all | solution.py:554
  8.9 12.2 %collective-permute-start.1 = (f32[240,128]{1,0:T(8,128)}, f32[240,128]{1,0:T(8,128)S(1)}, u32[]{:S(2)}, u32[]{:S(2)}) collective-permute-start(f32[240,128]{1,0:T(8,128)} %bitcast.31), channel_id=1, source_target_pairs={{0,28},{4,0},{8,4},{12,8},{16,12},{20,16},{24,20},{28,24},{1,29},{... | collective-permute-start | bytes 368648 | tf_op jit(solution)/shard_map/ppermute | solution.py:550
  10.8 10.3 %collective-permute-start = (f32[240,128]{1,0:T(8,128)}, f32[240,128]{1,0:T(8,128)S(1)}, u32[]{:S(2)}, u32[]{:S(2)}) collective-permute-start(f32[240,128]{1,0:T(8,128)} %bitcast.32), channel_id=1, source_target_pairs={{0,4},{4,8},{8,12},{12,16},{16,20},{20,24},{24,28},{28,0},{1,5},{5... | collective-permute-start | bytes 368648 | tf_op jit(solution)/shard_map/ppermute | solution.py:550
  10.8 9.5 %collective-permute-start.2 = (f32[8,128]{1,0:T(8,128)S(1)}, f32[8,128]{1,0:T(8,128)S(1)}, u32[]{:S(2)}, u32[]{:S(2)}) collective-permute-start(f32[8,128]{1,0:T(8,128)S(1)} %get-tuple-element.31), channel_id=1, source_target_pairs={{0,1},{1,2},{2,3},{3,0},{4,5},{5,6},{6,7},{7,4},{8,9},{9,10},{10,1... | collective-permute-start | bytes 12296 | tf_op jit(solution)/shard_map/ppermute | solution.py:550
  14.4 6.7 %collective-permute-start.3 = (f32[8,128]{1,0:T(8,128)S(1)}, f32[8,128]{1,0:T(8,128)S(1)}, u32[]{:S(2)}, u32[]{:S(2)}) collective-permute-start(f32[8,128]{1,0:T(8,128)S(1)} %get-tuple-element.32), channel_id=1, source_target_pairs={{0,3},{1,0},{2,1},{3,2},{4,7},{5,4},{6,5},{7,6},{8,11},{9,8},{10,9... | collective-permute-start | bytes 12296 | tf_op jit(solution)/shard_map/ppermute | solution.py:550
  51.3 11.6 %collective-permute-start.5 = (f32[240,128]{1,0:T(8,128)S(1)}, f32[240,128]{1,0:T(8,128)S(1)}, u32[]{:S(2)}, u32[]{:S(2)}) collective-permute-start(f32[240,128]{1,0:T(8,128)S(1)} %get-tuple-element.46.x_ref.refs_0_), channel_id=1, source_target_pairs={{0,28},{4,0},{8,4},{12,8},{16,12},{20,16},{24,20},{28,24},{1,29},{... | collective-permute-start | bytes 368648 | tf_op jit(solution)/shard_map/ppermute | solution.py:550
  52.7 10.2 %collective-permute-start.4 = (f32[240,128]{1,0:T(8,128)S(1)}, f32[240,128]{1,0:T(8,128)S(1)}, u32[]{:S(2)}, u32[]{:S(2)}) collective-permute-start(f32[240,128]{1,0:T(8,128)S(1)} %get-tuple-element.46.x_ref.refs_0_), channel_id=1, source_target_pairs={{0,4},{4,8},{8,12},{12,16},{16,20},{20,24},{24,28},{28,0},{1,5},{5... | collective-permute-start | bytes 368648 | tf_op jit(solution)/shard_map/ppermute | solution.py:550
  52.7 7.5 %collective-permute-start.6 = (f32[8,128]{1,0:T(8,128)S(1)}, f32[8,128]{1,0:T(8,128)S(1)}, u32[]{:S(2)}, u32[]{:S(2)}) collective-permute-start(f32[8,128]{1,0:T(8,128)S(1)} %get-tuple-element.47), channel_id=1, source_target_pairs={{0,1},{1,2},{2,3},{3,0},{4,5},{5,6},{6,7},{7,4},{8,9},{9,10},{10,1... | collective-permute-start | bytes 12296 | tf_op jit(solution)/shard_map/ppermute | solution.py:550
  56.2 6.7 %collective-permute-start.7 = (f32[8,128]{1,0:T(8,128)S(1)}, f32[8,128]{1,0:T(8,128)S(1)}, u32[]{:S(2)}, u32[]{:S(2)}) collective-permute-start(f32[8,128]{1,0:T(8,128)S(1)} %get-tuple-element.48), channel_id=1, source_target_pairs={{0,3},{1,0},{2,1},{3,2},{4,7},{5,4},{6,5},{7,6},{8,11},{9,8},{10,9... | collective-permute-start | bytes 12296 | tf_op jit(solution)/shard_map/ppermute | solution.py:550
